TPU v7x, 32 devices: a whole 2x2x4 slice. The times are simulated.
32 devices in a mesh: snap: 4 (over x, core), param: 8 (over z, y).
Axes of the slice: x: 2, y: 2, z: 4, core: 2. Of those that a mesh axis runs over, the one named last changes fastest.
Arguments:
- snap_in: float32 [32, 64, 1344], P('snap', None, 'param'), may hold values from -6 to 6
- snap_qkv: float32 [32, 1344, 4032], P('snap', 'param'), may hold values from -6 to 6
- snap_proj: float32 [32, 1344, 1344], P('snap', 'param'), may hold values from -6 to 6
- snap_out: float32 [32, 1344, 64], P('snap', 'param'), may hold values from -48 to 48
- coeffs: float32 [32, 8], P('snap'), may hold values from -3 to 3
- latent: float32 [8, 64, 256], P('param'), may hold values from -6 to 6
- levels: int32 [8], P('param'), may hold values from 0 to 15
Outputs:
- denoised: float32 [8, 8, 64, 256], P('snap', 'param')
All inputs are finite; a program needn't handle non-finite values.
Results may differ from a plain program's by a relative error of at most 0.012.
Values may be sent and summed in bfloat16 or wider, within the bound.
A program may use at most 192 MiB of HBM per device.

v0:
```python
import jax
import jax.numpy as jnp
from jax import lax
from jax.sharding import PartitionSpec as P

HEAD_DIM = 64
PROF = 8
NLEV = 16


EPS = 0.0001


def noise_scales(levels):
    step = levels.astype(jnp.float32) / (NLEV - 1)
    sigma = jnp.exp(jnp.log(0.2) + step * (jnp.log(5.0) - jnp.log(0.2)))
    square = sigma * sigma + 0.25
    return (1.0 / jnp.sqrt(square), 0.25 / square, 0.5 * sigma / jnp.sqrt(square))


def to_tokens(image):
    count = image.shape[0]
    parts = image.reshape(count, 16, 4, 16, 4, 4).transpose(0, 1, 3, 2, 4, 5)
    return parts.reshape(count, 256, 64)


def from_tokens(feature):
    count = feature.shape[0]
    parts = feature.reshape(count, 16, 16, 4, 4, 4).transpose(0, 1, 3, 2, 4, 5)
    return parts.reshape(count, 64, 256)


def head_unit(values):
    scale = jnp.sqrt(jnp.mean(values * values, axis=-1, keepdims=True))
    return (values / (EPS + scale)).astype(jnp.bfloat16)


def contract(coeffs, snaps):
    return jnp.einsum("sp,sij->pij", coeffs, snaps, precision=lax.Precision.HIGHEST)


def squares(weights):
    return jnp.sum(weights * weights, axis=1)


def scaled(weights, sums):
    return (weights / (EPS + jnp.sqrt(sums))[:, None, :]).astype(jnp.bfloat16)


def denoise(tokens, w_in, qkv_product, proj_product, w_out):
    rows = tokens.shape[0]
    count = rows // 256
    width = w_in.shape[1]
    heads = width // HEAD_DIM
    hidden = jnp.dot(tokens, w_in, preferred_element_type=jnp.float32).astype(jnp.bfloat16)
    qkv = qkv_product(hidden)
    qkv = head_unit(qkv.reshape(count, 256, 3, heads, HEAD_DIM))
    query = qkv[:, :, 0]
    keys = qkv[:, :, 1]
    values = qkv[:, :, 2]
    scores = jnp.einsum("bqhd,bkhd->bhqk", query, keys, preferred_element_type=jnp.float32)
    scores = scores * (1.0 / jnp.sqrt(float(HEAD_DIM)))
    expo = jnp.exp(scores)
    weights = (expo / jnp.sum(expo, axis=-1, keepdims=True)).astype(jnp.bfloat16)
    attended = jnp.einsum("bhqk,bkhd->bqhd", weights, values, preferred_element_type=jnp.float32)
    attended = attended.astype(jnp.bfloat16).reshape(rows, width)
    projected = proj_product(attended)
    mixed = ((0.7 * hidden.astype(jnp.float32) + 0.3 * projected) / jnp.sqrt(0.58)).astype(
        jnp.bfloat16
    )
    return jnp.dot(mixed, w_out, preferred_element_type=jnp.float32)


def prepare(latent, levels):
    c_in, c_skip, c_out = noise_scales(levels)
    count = latent.shape[0]
    tokens = to_tokens(c_in[:, None, None] * latent).reshape(count * 256, 64).astype(jnp.bfloat16)
    return (tokens, c_skip, c_out)


def finish(feature, latent, c_skip, c_out):
    count = latent.shape[0]
    image = from_tokens(feature.reshape(count, 256, 64))
    return c_skip[:, None, None] * latent + c_out[:, None, None] * image


def plain_products(full_qkv, full_proj):

    def qkv_product(hidden):
        return jnp.dot(hidden, full_qkv, preferred_element_type=jnp.float32)

    def proj_product(attended):
        return jnp.dot(attended, full_proj, preferred_element_type=jnp.float32)

    return (qkv_product, proj_product)


def one_group_profile(unit_in, unit_qkv, unit_proj, unit_out, tokens, latent, c_skip, c_out):
    full_in, full_qkv, full_proj, full_out = (
        lax.all_gather(unit_in, "param", axis=1, tiled=True),
        lax.all_gather(unit_qkv, "param", axis=0, tiled=True),
        lax.all_gather(unit_proj, "param", axis=0, tiled=True),
        lax.all_gather(unit_out, "param", axis=0, tiled=True),
    )
    qkv_product, proj_product = plain_products(full_qkv, full_proj)
    feature = denoise(tokens, full_in, qkv_product, proj_product, full_out)
    return finish(feature, latent, c_skip, c_out)


def shards(snap_in, snap_qkv, snap_proj, snap_out, coeffs, latent, levels):
    owned = PROF // lax.axis_size("snap")
    part_in = contract(coeffs, snap_in)
    part_qkv = contract(coeffs, snap_qkv)
    part_proj = contract(coeffs, snap_proj)
    part_out = contract(coeffs, snap_out)
    prof_in, prof_qkv, prof_proj, prof_out = (
        lax.psum_scatter(
            part_in.astype(jnp.bfloat16), "snap", scatter_dimension=0, tiled=True
        ).astype(jnp.float32),
        lax.psum_scatter(
            part_qkv.astype(jnp.bfloat16), "snap", scatter_dimension=0, tiled=True
        ).astype(jnp.float32),
        lax.psum_scatter(
            part_proj.astype(jnp.bfloat16), "snap", scatter_dimension=0, tiled=True
        ).astype(jnp.float32),
        lax.psum_scatter(
            part_out.astype(jnp.bfloat16), "snap", scatter_dimension=0, tiled=True
        ).astype(jnp.float32),
    )
    sums_qkv, sums_proj, sums_out = lax.psum(
        (squares(prof_qkv), squares(prof_proj), squares(prof_out)), "param"
    )
    unit_in = scaled(prof_in, squares(prof_in))
    unit_qkv = scaled(prof_qkv, sums_qkv)
    unit_proj = scaled(prof_proj, sums_proj)
    unit_out = scaled(prof_out, sums_out)
    tokens, c_skip, c_out = prepare(latent, levels)
    results = []
    for profile in range(owned):
        results.append(
            one_group_profile(
                unit_in[profile],
                unit_qkv[profile],
                unit_proj[profile],
                unit_out[profile],
                tokens,
                latent,
                c_skip,
                c_out,
            )
        )
    return jnp.stack(results)


def solution(mesh):
    in_specs = (
        P("snap", None, "param"),
        P("snap", "param", None),
        P("snap", "param", None),
        P("snap", "param", None),
        P("snap", None),
        P("param", None, None),
        P("param"),
    )
    out_specs = P("snap", "param", None, None)
    return jax.shard_map(shards, mesh=mesh, in_specs=in_specs, out_specs=out_specs, check_vma=False)
```

profile of v0, /device:TPU:0, one launch (start us, length us, event | category | flops | bytes accessed | tf_op | source)
XLA Modules:
  0.0 710.4 jit_solution(3761133656801974842)
XLA Ops:
  6.5 1.0 copy-done
  7.6 1.5 convolution_convert_fusion.2
  9.9 10.5 %fusion.15 = bf16[8,168,1344]{2,0,1:T(8,128)(2,1)S(1)} fusion(f32[8,168,1344]{2,1,0:T(8,128)} %param.9, f32[8,8]{1,0:T(8,128)} %param.11), kind=kOutput, calls=%fused_computation.19 | convolution fusion | flops 175214592 | bytes 10838272 | tf_op jit(solution)/shard_map/sp,sij->pij/dot_general | solution.py:39
  20.4 2.4 copy.50
  23.5 37.1 %fusion.6 = bf16[8,168,4032]{2,0,1:T(8,128)(2,1)S(1)} fusion(f32[8,168,4032]{2,1,0:T(8,128)} %param.8, f32[8,8]{1,0:T(8,128)S(1)} %copy-done.9), kind=kOutput, calls=%fused_computation.6 | convolution fusion | flops 525643776 | bytes 32514304 | tf_op jit(solution)/shard_map/sp,sij->pij/dot_general | solution.py:39
  60.6 16.2 %copy.46 = bf16[8,168,4032]{2,1,0:T(8,128)(2,1)} copy(bf16[8,168,4032]{2,0,1:T(8,128)(2,1)S(1)} %fusion.6) | data formatting | bytes 21676032 | tf_op jit(solution)/shard_map/convert_element_type | solution.py:121
  80.6 1.4 fusion.48
  82.0 86.8 %reduce-scatter.7.cloned.1.call-done = bf16[2,168,4032]{2,1,0:T(8,128)(2,1)} async-done(((bf16[8,168,4032]{2,1,0:T(8,128)(2,1)}), bf16[2,168,4032]{2,1,0:T(8,128)(2,1)}) %reduce-scatter.7.cloned.1.call-update) | async-done | bytes 2709520 | tf_op jit(solution)/shard_map/reduce_scatter | solution.py:120
  168.8 2.5 fusion.11
  171.4 37.5 %all-reduce = (f32[2,4032]{1,0:T(2,128)S(1)}, f32[2,1344]{1,0:T(2,128)S(1)}, f32[2,64]{1,0:T(2,128)S(1)}) all-reduce(f32[2,4032]{1,0:T(2,128)S(1)} %fusion.11, f32[2,1344]{1,0:T(2,128)S(1)} %fusion.48, f32[2,64]{1,0:T(2,128)S(1)} %fusion.80), channel_id=1, replica_groups=mesh['snap'=4,'param'=8] {'param'}, use_global_device_ids=true, to_apply=%region_4.0 | all-reduce | flops 10880 | bytes 87040 | tf_op jit(solution)/shard_map/psum | solution.py:130
  209.7 1.7 fusion.94
  215.6 1.2 convert_element_type.119
  216.8 2.0 copy.38
  221.0 34.1 %all-gather.4 = bf16[1,64,1344]{1,0,2:T(2,128)(2,1)S(1)} all-gather(bf16[1,64,168]{1,0,2:T(2,128)(2,1)S(1)} %copy.57), channel_id=6, replica_groups=mesh['snap'=4,'param'=8] {'param'}, dimensions={2}, use_global_device_ids=true | all-gather | bytes 193536 | tf_op jit(solution)/shard_map/all_gather | solution.py:100
  256.0 34.0 %all-gather = bf16[1,64,1344]{1,0,2:T(2,128)(2,1)S(1)} all-gather(bf16[1,64,168]{1,0,2:T(2,128)(2,1)S(1)} %copy.42), channel_id=2, replica_groups=mesh['snap'=4,'param'=8] {'param'}, dimensions={2}, use_global_device_ids=true | all-gather | bytes 193536 | tf_op jit(solution)/shard_map/all_gather | solution.py:100
  291.9 34.8 %all-gather.7 = bf16[1,1344,64]{2,0,1:T(2,128)(2,1)S(1)} all-gather(bf16[1,168,64]{2,0,1:T(2,128)(2,1)S(1)} %copy.60), channel_id=9, replica_groups=mesh['snap'=4,'param'=8] {'param'}, dimensions={1}, use_global_device_ids=true | all-gather | bytes 193536 | tf_op jit(solution)/shard_map/all_gather | solution.py:103
  327.6 33.6 %all-gather.3 = bf16[1,1344,64]{2,0,1:T(2,128)(2,1)S(1)} all-gather(bf16[1,168,64]{2,0,1:T(2,128)(2,1)S(1)} %copy.54), channel_id=5, replica_groups=mesh['snap'=4,'param'=8] {'param'}, dimensions={1}, use_global_device_ids=true | all-gather | bytes 193536 | tf_op jit(solution)/shard_map/all_gather | solution.py:103
  361.1 1.6 copy.55
  362.8 36.8 %all-gather.17.cloned.1.call-done = bf16[1,1344,4032]{2,1,0:T(8,128)(2,1)} async-done(((bf16[1,168,4032]{2,1,0:T(8,128)(2,1)}), bf16[1,1344,4032]{2,1,0:T(8,128)(2,1)}) %all-gather.17.cloned.1.call-update) | async-done | bytes 10838032 | tf_op jit(solution)/shard_map/all_gather | solution.py:101
  399.5 7.6 %fusion.2 = f32[256,4032]{0,1:T(8,128)S(1)} fusion(bf16[256,1344]{0,1:T(8,128)(2,1)S(1)} %convolution_convert_fusion, bf16[1,1344,4032]{2,1,0:T(8,128)(2,1)} %all-gather.17.cloned.1.call-done), kind=kOutput, calls=%fused_computation.2 | convolution fusion | flops 2774532096 | bytes 15654912 | tf_op jit(solution)/shard_map/dot_general | solution.py:90
  408.5 1.1 fusion.14
  409.6 1.1 fusion.50
  410.7 57.6 %all-gather.19.cloned.1.call-done = bf16[1,1344,1344]{2,1,0:T(8,128)(2,1)} async-done(((bf16[1,168,1344]{2,1,0:T(8,128)(2,1)}), bf16[1,1344,1344]{2,1,0:T(8,128)(2,1)}) %all-gather.19.cloned.1.call-update) | async-done | bytes 3612688 | tf_op jit(solution)/shard_map/all_gather | solution.py:102
  468.3 3.9 fusion.61
  472.4 2.0 copy.62
  475.4 151.0 %all-gather.13.cloned.1.call-done = bf16[1,1344,4032]{2,1,0:T(8,128)(2,1)} async-done(((bf16[1,168,4032]{2,1,0:T(8,128)(2,1)}), bf16[1,1344,4032]{2,1,0:T(8,128)(2,1)}) %all-gather.13.cloned.1.call-update) | async-done | bytes 10838032 | tf_op jit(solution)/shard_map/all_gather | solution.py:101
  626.4 7.8 %fusion.4 = f32[256,4032]{0,1:T(8,128)S(1)} fusion(bf16[256,1344]{0,1:T(8,128)(2,1)S(1)} %convolution_convert_fusion.1, bf16[1,1344,4032]{2,1,0:T(8,128)(2,1)} %all-gather.13.cloned.1.call-done), kind=kOutput, calls=%fused_computation.4 | convolution fusion | flops 2774532096 | bytes 15654912 | tf_op jit(solution)/shard_map/dot_general | solution.py:90
  635.6 1.1 fusion.13
  636.7 1.1 fusion.51
  637.8 57.5 %all-gather.15.cloned.1.call-done = bf16[1,1344,1344]{2,1,0:T(8,128)(2,1)} async-done(((bf16[1,168,1344]{2,1,0:T(8,128)(2,1)}), bf16[1,1344,1344]{2,1,0:T(8,128)(2,1)}) %all-gather.15.cloned.1.call-update) | async-done | bytes 3612688 | tf_op jit(solution)/shard_map/all_gather | solution.py:102
  695.3 3.9 fusion.58
  699.5 2.0 copy.56
  (80 shorter events, 21.0 us)
Async XLA Ops:
  6.5 1.0 copy-start
  6.5 73.0 %reduce-scatter.11.cloned.1.call-start = ((), (), s32[]{:S(2)}) async-start(), calls=%async_computation.7 | async-start | bytes 327680 | tf_op jit(solution)/shard_map/reduce_scatter | solution.py:126
  9.9 70.7 %reduce-scatter.9.cloned.1.call-start = ((), (), s32[]{:S(2)}) async-start(), calls=%async_computation.6 | async-start | bytes 4730880 | tf_op jit(solution)/shard_map/reduce_scatter | solution.py:123
  22.8 0.7 copy-start.9
  22.8 146.0 %reduce-scatter.7.cloned.1.call-start = ((), (), s32[]{:S(2)}) async-start(), calls=%async_computation.5 | async-start | bytes 13762560 | tf_op jit(solution)/shard_map/reduce_scatter | solution.py:120
  76.8 1.1 copy-start.4
  76.9 142.3 %reduce-scatter.5.cloned.1.call-start = ((), (), s32[]{:S(2)}) async-start(), calls=%async_computation.4 | async-start | bytes 327680 | tf_op jit(solution)/shard_map/reduce_scatter | solution.py:117
  79.5 320.0 %all-gather.17.cloned.1.call-start = ((), (), s32[]{:S(2)}) async-start(), calls=%async_computation.10 | async-start | bytes 12386304 | tf_op jit(solution)/shard_map/all_gather | solution.py:101
  168.8 40.1 %copy-start.2 = (bf16[2,168,4032]{2,1,0:T(8,128)(2,1)S(1)}, bf16[2,168,4032]{2,1,0:T(8,128)(2,1)}, u32[]{:S(2)}) copy-start(bf16[2,168,4032]{2,1,0:T(8,128)(2,1)} %reduce-scatter.7.cloned.1.call-done) | copy-start | bytes 8128516
  209.6 2.2 copy-start.3
  211.4 3.3 copy-start.6
  211.4 256.9 %all-gather.19.cloned.1.call-start = ((), (), s32[]{:S(2)}) async-start(), calls=%async_computation.11 | async-start | bytes 4257792 | tf_op jit(solution)/shard_map/all_gather | solution.py:102
  213.1 413.3 %all-gather.13.cloned.1.call-start = ((), (), s32[]{:S(2)}) async-start(), calls=%async_computation.8 | async-start | bytes 12386304 | tf_op jit(solution)/shard_map/all_gather | solution.py:101
  213.9 481.4 %all-gather.15.cloned.1.call-start = ((), (), s32[]{:S(2)}) async-start(), calls=%async_computation.9 | async-start | bytes 4257792 | tf_op jit(solution)/shard_map/all_gather | solution.py:102
  216.8 74.8 %copy-start.7 = (bf16[2,168,64]{1,2,0:T(8,128)(2,1)S(1)}, bf16[2,168,64]{1,2,0:T(8,128)(2,1)}, u32[]{:S(2)}) copy-start(bf16[2,168,64]{1,2,0:T(8,128)(2,1)} %reduce-scatter.11.cloned.1.call-done) | copy-start | bytes 129028
  636.7 58.6 %copy-start.8 = (bf16[1,1344,64]{1,2,0:T(8,128)(2,1)S(1)}, bf16[1,1344,64]{1,2,0:T(8,128)(2,1)}, u32[]{:S(2)}) copy-start(bf16[1,1344,64]{1,2,0:T(8,128)(2,1)} %copy.55) | copy-start | bytes 516100
  695.3 8.1 %copy-start.1 = (f32[8,168,64]{1,2,0:T(8,128)S(1)}, f32[8,168,64]{1,2,0:T(8,128)}, u32[]{:S(2)}) copy-start(f32[8,168,64]{1,2,0:T(8,128)} %param.10) | copy-start | bytes 1032196
  699.2 3.3 copy-start.5
Sparse Core Ops, SparseCore 0:
  10.0 22.7 reduce-scatter.10
  35.5 41.9 reduce-scatter.8
  80.1 88.7 reduce-scatter.6
  171.1 20.0 reduce-scatter.4
  211.5 187.9 all-gather.16
  401.8 66.4 all-gather.18
  470.7 155.6 all-gather.12
  628.9 66.4 all-gather.14
where the time goes:
time: 717 us; the launch traced here: 710 us
  waiting for transfers between devices  391 us (55%)
  blocking collectives  174 us (24%)
  matrix products  78.3 us (11%)
  local copies, waits for them, and re-layouts  41.4 us (6%)
  between operations  15 us (2%)
  other arithmetic  10.4 us (1%)
    all_gather x2, waiting for transfers between devices, one_group_profile(): lax.all_gather(unit_qkv, 'param', axis=0, tiled=True)  188 us
    all_gather x2, waiting for transfers between devices, one_group_profile(): lax.all_gather(unit_proj, 'param', axis=0, tiled=True)  115 us
    reduce_scatter x1, waiting for transfers between devices, shards(): lax.psum_scatter(part_qkv.astype(jnp.bfloat16), 'snap', scatter_dimension...  86.8 us
    all_gather x2, blocking collectives, one_group_profile(): lax.all_gather(unit_out, 'param', axis=0, tiled=True)  68.3 us
    all_gather x2, blocking collectives, one_group_profile(): lax.all_gather(unit_in, 'param', axis=1, tiled=True)  68 us
    dot_general x4, matrix products, contract(): jnp.einsum('sp,sij->pij', coeffs, snaps, precision=lax.Precision.HIGHEST)  49.9 us
    psum x1, blocking collectives, shards(): lax.psum((squares(prof_qkv), squares(prof_proj), squares(prof_out)), 'par...  37.5 us
    convert_element_type x1, local copies, waits for them, and re-layouts, shards(): part_qkv.astype(jnp.bfloat16)  16.2 us
  transfers between devices with their start and end apart: 8, of which 5 were waited for; matrix products, arithmetic and copies ran while one was open for 17% of the time, Pallas kernels for 0%

commit v1 on v0

v1 whole, which is shorter than its diff:
```python
import jax
import jax.numpy as jnp
from jax import lax
from jax.sharding import PartitionSpec as P

HEAD_DIM = 64
PROF = 8
NLEV = 16


EPS = 0.0001


def noise_scales(levels):
    step = levels.astype(jnp.float32) / (NLEV - 1)
    sigma = jnp.exp(jnp.log(0.2) + step * (jnp.log(5.0) - jnp.log(0.2)))
    square = sigma * sigma + 0.25
    return (1.0 / jnp.sqrt(square), 0.25 / square, 0.5 * sigma / jnp.sqrt(square))


def to_tokens(image):
    count = image.shape[0]
    parts = image.reshape(count, 16, 4, 16, 4, 4).transpose(0, 1, 3, 2, 4, 5)
    return parts.reshape(count, 256, 64)


def from_tokens(feature):
    count = feature.shape[0]
    parts = feature.reshape(count, 16, 16, 4, 4, 4).transpose(0, 1, 3, 2, 4, 5)
    return parts.reshape(count, 64, 256)


def head_unit(values):
    scale = jnp.sqrt(jnp.mean(values * values, axis=-1, keepdims=True))
    return (values / (EPS + scale)).astype(jnp.bfloat16)


def contract(coeffs, snaps):
    return jnp.einsum("sp,sij->pij", coeffs, snaps, precision=lax.Precision.HIGHEST)


def squares(weights):
    return jnp.sum(weights * weights, axis=1)


def inverse_norms(sums):
    return 1.0 / (EPS + jnp.sqrt(sums))


def attend(tokens, mixed_qkv, mixed_out, skip_map):
    rows = tokens.shape[0]
    count = rows // 256
    width = mixed_out.shape[0]
    heads = width // HEAD_DIM
    qkv = jnp.dot(tokens, mixed_qkv, preferred_element_type=jnp.float32)
    qkv = head_unit(qkv.reshape(count, 256, 3, heads, HEAD_DIM))
    query = qkv[:, :, 0]
    keys = qkv[:, :, 1]
    values = qkv[:, :, 2]
    scores = jnp.einsum("bqhd,bkhd->bhqk", query, keys, preferred_element_type=jnp.float32)
    scores = scores * (1.0 / jnp.sqrt(float(HEAD_DIM)))
    expo = jnp.exp(scores)
    weights = (expo / jnp.sum(expo, axis=-1, keepdims=True)).astype(jnp.bfloat16)
    attended = jnp.einsum("bhqk,bkhd->bqhd", weights, values, preferred_element_type=jnp.float32)
    attended = attended.astype(jnp.bfloat16).reshape(rows, width)
    skip = jnp.dot(tokens.astype(jnp.float32), skip_map, precision=lax.Precision.HIGHEST)
    mapped = jnp.dot(attended, mixed_out, preferred_element_type=jnp.float32)
    return (0.7 * skip + 0.3 * mapped) / jnp.sqrt(0.58)


def prepare(latent, levels):
    c_in, c_skip, c_out = noise_scales(levels)
    count = latent.shape[0]
    tokens = to_tokens(c_in[:, None, None] * latent).reshape(count * 256, 64).astype(jnp.bfloat16)
    return (tokens, c_skip, c_out)


def finish(feature, latent, c_skip, c_out):
    count = latent.shape[0]
    image = from_tokens(feature.reshape(count, 256, 64))
    return c_skip[:, None, None] * latent + c_out[:, None, None] * image


def reduced(coeffs, snaps):
    part = contract(coeffs, snaps).astype(jnp.bfloat16)
    return lax.psum_scatter(part, "snap", scatter_dimension=0, tiled=True).astype(jnp.float32)


def rows_product(left, right):
    return jnp.einsum("pfr,prc->pfc", left, right.astype(jnp.bfloat16), preferred_element_type=jnp.float32)


def shards(snap_in, snap_qkv, snap_proj, snap_out, coeffs, latent, levels):
    owned = PROF // lax.axis_size("snap")
    prof_in = reduced(coeffs, snap_in)
    prof_out = reduced(coeffs, snap_out)
    prof_proj = reduced(coeffs, snap_proj)
    prof_qkv = reduced(coeffs, snap_qkv)
    unit_in = (prof_in * inverse_norms(squares(prof_in))[:, None, :]).astype(jnp.bfloat16)
    full_out = lax.all_gather(prof_out, "param", axis=1, tiled=True)
    unit_out = full_out * inverse_norms(squares(full_out))[:, None, :]
    part_map = rows_product(unit_in, prof_qkv)
    part_skip = jnp.einsum(
        "pfr,prc->pfc", unit_in.astype(jnp.float32), prof_out, precision=lax.Precision.HIGHEST
    )
    sums_qkv, sums_proj, qkv_map, skip_map = lax.psum(
        (squares(prof_qkv), squares(prof_proj), part_map, part_skip), "param"
    )
    qkv_map = (qkv_map * inverse_norms(sums_qkv)[:, None, :]).astype(jnp.bfloat16)
    skip_map = skip_map * inverse_norms(squares(full_out))[:, None, :]
    scaled_out = (unit_out * inverse_norms(sums_proj)[:, :, None]).astype(jnp.bfloat16)
    own_rows = jnp.einsum(
        "prc,pcf->prf", prof_proj.astype(jnp.bfloat16), scaled_out, preferred_element_type=jnp.float32
    ).astype(jnp.bfloat16)
    out_map = lax.all_gather(own_rows, "param", axis=1, tiled=True)
    tokens, c_skip, c_out = prepare(latent, levels)
    results = []
    for profile in range(owned):
        feature = attend(tokens, qkv_map[profile], out_map[profile], skip_map[profile])
        results.append(finish(feature, latent, c_skip, c_out))
    return jnp.stack(results)


def solution(mesh):
    in_specs = (
        P("snap", None, "param"),
        P("snap", "param", None),
        P("snap", "param", None),
        P("snap", "param", None),
        P("snap", None),
        P("param", None, None),
        P("param"),
    )
    out_specs = P("snap", "param", None, None)
    return jax.shard_map(shards, mesh=mesh, in_specs=in_specs, out_specs=out_specs, check_vma=False)
```

time: 717 us -> 405 us (0.56)
  waiting for transfers between devices: 391 us -> 198 us
  blocking collectives: 174 us -> 72.1 us
  matrix products: 78.3 us -> 65.5 us
    all_gather x4 -> x0, waiting for transfers between devices: 303 us -> none  [the longest x2 188 us: one_group_profile(): lax.all_gather(unit_qkv, 'param', axis=0, tiled=True)]
    psum x0 -> x2, waiting for transfers between devices: none -> 138 us  [shards(): lax.psum((squares(prof_qkv), squares(prof_proj), part_map, part_skip), 'p...]
    all_gather x4 -> x2, blocking collectives: 136 us -> 72.1 us  [the longest x1 37.4 us: shards(): full_out = lax.all_gather(prof_out, 'param', axis=1, tiled=True)]
    psum x1 -> x0, blocking collectives: 37.5 us -> none  [shards(): lax.psum((squares(prof_qkv), squares(prof_proj), squares(prof_out)), 'par...]
    reduce_scatter x4, waiting for transfers between devices: 86.9 us -> 60.7 us  [reduced(): lax.psum_scatter(part, 'snap', scatter_dimension=0, tiled=True)]
    dot_general x10 -> x13, matrix products: 28.3 us -> 14.5 us  [the longest x2 3.43 us: attend(): qkv = jnp.dot(tokens, mixed_qkv, preferred_element_type=jnp.float32)]
    convert_element_type x4 -> x6, local copies, waits for them, and re-layouts: 20.1 us -> 21.2 us  [the longest x4 20.1 us: reduced(): part = contract(coeffs, snaps).astype(jnp.bfloat16)]
  transfers between devices with their start and end apart: 8 -> 6, of which waited for: 5 -> 3; matrix products, arithmetic and copies ran while one was open for 17% -> 22% of each run, Pallas kernels for 0% -> 0%
where the time goes in v1:
time: 405 us
  waiting for transfers between devices  198 us (49%)
  blocking collectives  72.1 us (18%)
  matrix products  65.5 us (16%)
  local copies, waits for them, and re-layouts  38.5 us (10%)
  other arithmetic  15.3 us (4%)
  between operations  14.7 us (4%)
    psum x2, waiting for transfers between devices, shards(): lax.psum((squares(prof_qkv), squares(prof_proj), part_map, part_skip), 'p...  138 us
    reduce_scatter x4, waiting for transfers between devices, reduced(): lax.psum_scatter(part, 'snap', scatter_dimension=0, tiled=True)  60.7 us
    dot_general x4, matrix products, contract(): jnp.einsum('sp,sij->pij', coeffs, snaps, precision=lax.Precision.HIGHEST)  51 us
    all_gather x1, blocking collectives, shards(): full_out = lax.all_gather(prof_out, 'param', axis=1, tiled=True)  37.4 us
    all_gather x1, blocking collectives, shards(): out_map = lax.all_gather(own_rows, 'param', axis=1, tiled=True)  34.8 us
    convert_element_type x4, local copies, waits for them, and re-layouts, reduced(): part = contract(coeffs, snaps).astype(jnp.bfloat16)  20.1 us
  transfers between devices with their start and end apart: 6, of which 3 were waited for; matrix products, arithmetic and copies ran while one was open for 22% of the time, Pallas kernels for 0%

profile of v1, /device:TPU:0, one launch (start us, length us, event | category | flops | bytes accessed | tf_op | source)
XLA Modules:
  0.0 404.8 jit_solution(6215788751018929233)
XLA Ops:
  6.5 1.0 copy-done
  7.6 1.5 convolution_convert_fusion
  9.9 1.9 convolution_convert_fusion.1
  12.6 10.5 %fusion.9 = bf16[8,168,1344]{2,0,1:T(8,128)(2,1)S(1)} fusion(f32[8,168,1344]{2,1,0:T(8,128)} %param.9, f32[8,8]{1,0:T(8,128)} %param.11), kind=kOutput, calls=%fused_computation.12 | convolution fusion | flops 175214592 | bytes 10838272 | tf_op jit(solution)/shard_map/sp,sij->pij/dot_general | solution.py:39
  23.1 2.4 copy.140
  25.7 37.2 %fusion.2 = bf16[8,168,4032]{2,0,1:T(8,128)(2,1)S(1)} fusion(f32[8,168,4032]{2,1,0:T(8,128)} %param.8, f32[8,8]{1,0:T(8,128)S(1)} %copy-done.8), kind=kOutput, calls=%fused_computation.2 | convolution fusion | flops 525643776 | bytes 32514304 | tf_op jit(solution)/shard_map/sp,sij->pij/dot_general | solution.py:39
  62.9 16.2 %copy.136 = bf16[8,168,4032]{2,1,0:T(8,128)(2,1)} copy(bf16[8,168,4032]{2,0,1:T(8,128)(2,1)S(1)} %fusion.2) | data formatting | bytes 21676032 | tf_op jit(solution)/shard_map/convert_element_type | solution.py:85
  80.3 1.2 convert_element_type.109
  81.5 2.0 copy.126
  84.8 37.4 %all_gather.6 = f32[2,1344,64]{2,0,1:T(2,128)S(1)} all-gather(f32[2,168,64]{2,0,1:T(2,128)S(1)} %copy.133), channel_id=1, replica_groups=mesh['snap'=4,'param'=8] {'param'}, dimensions={1}, use_global_device_ids=true | all-gather | bytes 774144 | tf_op jit(solution)/shard_map/all_gather | solution.py:100
  122.2 2.2 copy.141
  125.4 1.4 multiply_reduce_fusion.4
  126.8 1.6 fusion.34
  128.5 2.3 multiply_reduce_fusion.3
  130.8 60.6 %reduce-scatter.9.cloned.1.call-done = bf16[2,168,4032]{2,1,0:T(8,128)(2,1)} async-done(((bf16[8,168,4032]{2,1,0:T(8,128)(2,1)}), bf16[2,168,4032]{2,1,0:T(8,128)(2,1)}) %reduce-scatter.9.cloned.1.call-update) | async-done | bytes 2709520 | tf_op jit(solution)/shard_map/reduce_scatter | solution.py:86
  191.4 3.2 multiply_reduce_fusion
  194.6 2.0 fusion.32
  196.7 68.2 %all-reduce.6.cloned.1.call-done = (f32[2,64,64]{2,1,0:T(8,128)}, f32[2,4032]{1,0:T(2,128)}, f32[2,1344]{1,0:T(2,128)}) async-done(((f32[2,64,64]{2,1,0:T(8,128)}, f32[2,4032]{1,0:T(2,128)}, f32[2,1344]{1,0:T(2,128)}), (f32[2,64,64]{2,1,0:T(8,128)}, f32[2,4032]{1,0:T(2,128)}, f32[2,1344]{1,0:T(2,128)})) %all-reduce.6.cloned.1.call-update) | async-done | bytes 75792 | tf_op jit(solution)/shard_map/psum | solution.py:106
  265.6 1.9 convolution_convert_fusion.2
  267.6 34.8 %all_gather.7 = bf16[2,1344,64]{2,0,1:T(2,128)(2,1)S(1)} all-gather(bf16[2,168,64]{2,0,1:T(2,128)(2,1)S(1)} %copy.142), channel_id=1, replica_groups=mesh['snap'=4,'param'=8] {'param'}, dimensions={1}, use_global_device_ids=true | all-gather | bytes 387072 | tf_op jit(solution)/shard_map/all_gather | solution.py:115
  305.6 69.4 %all-reduce.4.cloned.1.call-done = f32[2,64,4032]{2,1,0:T(8,128)} async-done(((f32[2,64,4032]{2,1,0:T(8,128)}), f32[2,64,4032]{2,1,0:T(8,128)}) %all-reduce.4.cloned.1.call-update) | async-done | bytes 2064400 | tf_op jit(solution)/shard_map/psum | solution.py:106
  375.0 1.8 multiply_convert_fusion
  377.6 2.7 fusion.23
  381.5 1.2 fusion.8
  382.7 1.1 fusion.14
  384.2 2.0 copy.147
  386.2 1.0 mul.221
  387.3 2.9 multiply_reduce_fusion.2
  391.3 1.2 fusion.7
  392.5 1.1 fusion.15
  394.0 2.0 copy.144
  396.1 1.0 mul.213
  (66 shorter events, 13.3 us)
Async XLA Ops:
  6.5 1.0 copy-start
  6.5 77.2 %reduce-scatter.7.cloned.1.call-start = ((), (), s32[]{:S(2)}) async-start(), calls=%async_computation.5 | async-start | bytes 327680 | tf_op jit(solution)/shard_map/reduce_scatter | solution.py:86
  9.9 114.6 %reduce-scatter.5.cloned.1.call-start = ((), (), s32[]{:S(2)}) async-start(), calls=%async_computation.4 | async-start | bytes 327680 | tf_op jit(solution)/shard_map/reduce_scatter | solution.py:86
  12.6 115.9 %reduce-scatter.11.cloned.1.call-start = ((), (), s32[]{:S(2)}) async-start(), calls=%async_computation.8 | async-start | bytes 4730880 | tf_op jit(solution)/shard_map/reduce_scatter | solution.py:86
  23.1 2.7 copy-start.8
  25.5 165.9 %reduce-scatter.9.cloned.1.call-start = ((), (), s32[]{:S(2)}) async-start(), calls=%async_computation.6 | async-start | bytes 13762560 | tf_op jit(solution)/shard_map/reduce_scatter | solution.py:86
  79.1 0.9 copy-start.5
  79.2 185.7 %all-reduce.6.cloned.1.call-start = ((), (), s32[]{:S(2)}) async-start(), calls=%async_computation.9 | async-start | bytes 219136 | tf_op jit(solution)/shard_map/psum | solution.py:106
  83.8 43.1 %copy-start.6 = (bf16[2,168,64]{1,2,0:T(8,128)(2,1)S(1)}, bf16[2,168,64]{1,2,0:T(8,128)(2,1)}, u32[]{:S(2)}) copy-start(bf16[2,168,64]{1,2,0:T(8,128)(2,1)} %reduce-scatter.7.cloned.1.call-done) | copy-start | bytes 129028
  124.4 70.2 %copy-start.4 = (bf16[2,64,168]{2,1,0:T(8,128)(2,1)S(1)}, bf16[2,64,168]{2,1,0:T(8,128)(2,1)}, u32[]{:S(2)}) copy-start(bf16[2,64,168]{2,1,0:T(8,128)(2,1)} %reduce-scatter.5.cloned.1.call-done) | copy-start | bytes 129028
  191.4 3.2 copy-start.3
  194.6 180.5 %all-reduce.4.cloned.1.call-start = ((), (), s32[]{:S(2)}) async-start(), calls=%async_computation.7 | async-start | bytes 4194304 | tf_op jit(solution)/shard_map/psum | solution.py:106
  264.9 40.2 %copy-start.7 = (f32[2,64,64]{2,1,0:T(8,128)S(1)}, f32[2,64,64]{2,1,0:T(8,128)}, u32[]{:S(2)}) copy-start(f32[2,64,64]{2,1,0:T(8,128)} %get-tuple-element.5) | copy-start | bytes 98308
  264.9 40.7 %copy-start.9 = (f32[2,4032]{1,0:T(2,128)S(1)}, f32[2,4032]{1,0:T(2,128)}, u32[]{:S(2)}) copy-start(f32[2,4032]{1,0:T(2,128)} %get-tuple-element.6) | copy-start | bytes 96772
  387.3 3.4 copy-start.2
  392.5 5.5 %copy-start.1 = (f32[8,168,64]{1,2,0:T(8,128)S(1)}, f32[8,168,64]{1,2,0:T(8,128)}, u32[]{:S(2)}) copy-start(f32[8,168,64]{1,2,0:T(8,128)} %param.10) | copy-start | bytes 1032196
Sparse Core Ops, SparseCore 0:
  10.0 22.7 reduce-scatter.6
  35.3 20.0 reduce-scatter.4
  58.0 41.9 reduce-scatter.10
  102.6 88.7 reduce-scatter.8
  195.3 69.5 all-reduce.5
  268.3 106.6 all-reduce.3

commit v2 on v1

--- a/solution.py
+++ b/solution.py
@@ -1,6 +1,10 @@
+import functools
+
 import jax
 import jax.numpy as jnp
 from jax import lax
+from jax.experimental import pallas as pl
+from jax.experimental.pallas import tpu as pltpu
 from jax.sharding import PartitionSpec as P
 
 HEAD_DIM = 64
@@ -33,14 +37,6 @@
 def head_unit(values):
     scale = jnp.sqrt(jnp.mean(values * values, axis=-1, keepdims=True))
     return (values / (EPS + scale)).astype(jnp.bfloat16)
-
-
-def contract(coeffs, snaps):
-    return jnp.einsum("sp,sij->pij", coeffs, snaps, precision=lax.Precision.HIGHEST)
-
-
-def squares(weights):
-    return jnp.sum(weights * weights, axis=1)
 
 
 def inverse_norms(sums):
@@ -81,38 +77,399 @@
     return c_skip[:, None, None] * latent + c_out[:, None, None] * image
 
 
-def reduced(coeffs, snaps):
-    part = contract(coeffs, snaps).astype(jnp.bfloat16)
-    return lax.psum_scatter(part, "snap", scatter_dimension=0, tiled=True).astype(jnp.float32)
-
-
-def rows_product(left, right):
-    return jnp.einsum("pfr,prc->pfc", left, right.astype(jnp.bfloat16), preferred_element_type=jnp.float32)
+LANES = 128
+SUB = 8
+PIECE = 256
+
+
+def cut(width, pieces):
+    tiles = width // LANES
+    sizes = [tiles // pieces + (1 if i < tiles % pieces else 0) for i in range(pieces)]
+    return [size * LANES for size in sizes if size]
+
+
+def exchange_kernel(
+    cuts, proj_count, n, groups, real,
+    coeffs, aux, proj, qkv,
+    *refs,
+):
+    total = len(cuts)
+    maps = total - proj_count
+    pos = 0
+
+    def take(count):
+        nonlocal pos
+        pos += count
+        return refs[pos - count:pos]
+
+    k_out = take(maps)
+    (m_out, skip_out) = take(2)
+    (feed,) = take(1)
+    away, keep, near, over, far = (take(total) for _ in range(5))
+    g_send, g_recv, q_send, q_recv = (take(maps) for _ in range(4))
+    (aux_all, proj_w, proj_sq, proj_sq_in, unit_rows) = take(5)
+    (feed_sem, near_sems, far_sems, map_sems, aux_sems, sq_sems, m_sems) = take(7)
+
+    rows = groups * 2 * SUB
+    snap = lax.axis_index("snap")
+    me = lax.axis_index("param")
+    core = lax.rem(snap, 2)
+    sibling = snap + 1 - 2 * core
+    across = lax.rem(snap + 2, 4)
+
+    def peer(step):
+        return {"snap": snap, "param": lax.rem(me + step, n)}
+
+    barrier = pltpu.get_barrier_semaphore()
+    for other in (sibling, across):
+        pl.semaphore_signal(
+            barrier, inc=1, device_id={"snap": other, "param": me},
+            device_id_type=pl.DeviceIdType.MESH,
+        )
+
+    def greet(step, carry):
+        pl.semaphore_signal(
+            barrier, inc=1, device_id=peer(step), device_id_type=pl.DeviceIdType.MESH
+        )
+        return carry
+
+    lax.fori_loop(1, n, greet, 0)
+
+    sources = []
+    offset = 0
+    sources.append((aux, 0))
+    for index in range(1, total):
+        if index <= proj_count:
+            sources.append((proj, offset))
+        else:
+            sources.append((qkv, offset))
+        offset += cuts[index]
+        if index == proj_count:
+            offset = 0
+
+    def fetch(index):
+        source, start = sources[index]
+        slot = index % 2
+        return pltpu.make_async_copy(
+            source.at[:, :, start:start + cuts[index]],
+            feed.at[slot, :, :, 0:cuts[index]],
+            feed_sem.at[slot],
+        )
+
+    def remote(source, target, sems, at, device):
+        return pltpu.make_async_remote_copy(
+            src_ref=source, dst_ref=target, send_sem=sems.at[(0,) + at], recv_sem=sems.at[(1,) + at],
+            device_id=device, device_id_type=pl.DeviceIdType.MESH,
+        )
+
+    def near_copy(index):
+        return remote(away[index], near[index], near_sems, (index,), {"snap": sibling, "param": me})
+
+    def far_copy(index):
+        return remote(over[index], far[index], far_sems, (index,), {"snap": across, "param": me})
+
+    def each_peer(act):
+        def body(step, carry):
+            act(step)
+            return carry
+
+        lax.fori_loop(1, n, body, 0)
+
+    def map_copies(index, step):
+        goal = lax.rem(me + step, n)
+        half = (goal * 2) // n
+        return (
+            remote(g_send[index].at[goal], g_recv[index].at[step], map_sems, (index, 0, step), peer(step)),
+            remote(q_send[index].at[half], q_recv[index].at[step], map_sems, (index, 1, step), peer(step)),
+        )
+
+    def map_spread(index, step):
+        return remote(
+            k_out[index].at[me], k_out[index].at[me], map_sems, (index, 2, step), peer(step)
+        )
+
+    def aux_copy(step):
+        return remote(aux_all.at[me], aux_all.at[me], aux_sems, (step,), peer(step))
+
+    def sq_copy(step):
+        return remote(proj_sq, proj_sq_in.at[step], sq_sems, (step,), peer(step))
+
+    def m_copy(step):
+        return remote(m_out.at[me], m_out.at[me], m_sems, (step,), peer(step))
+
+    def contract(index):
+        width = cuts[index]
+        slot = index % 2
+
+        def body(group, carry):
+            at = pl.ds(pl.multiple_of(group * SUB, SUB), SUB)
+            to = pl.ds(pl.multiple_of(group * 2 * SUB, 2 * SUB), 2 * SUB)
+            for start in range(0, width, PIECE):
+                lanes = slice(start, min(start + PIECE, width))
+                snaps = [feed[slot, s, at, lanes] for s in range(feed.shape[1])]
+                for pair in range(4):
+                    both = []
+                    for column in (2 * pair, 2 * pair + 1):
+                        value = coeffs[0, column] * snaps[0]
+                        for s in range(1, len(snaps)):
+                            value = value + coeffs[s, column] * snaps[s]
+                        both.append(value)
+                    packed = jnp.concatenate(both, axis=0).astype(jnp.bfloat16)
+                    if pair < 2:
+                        keep[index][pair, to, lanes] = packed
+                    else:
+                        away[index][pair - 2, to, lanes] = packed
+            return carry
+
+        lax.fori_loop(0, groups, body, 0)
+
+    def pass_on(index):
+        near_copy(index).wait_recv()
+
+        def body(group, carry):
+            to = pl.ds(pl.multiple_of(group * 2 * SUB, 2 * SUB), 2 * SUB)
+            own = keep[index][1, to, :].astype(jnp.float32) + near[index][1, to, :].astype(jnp.float32)
+            over[index][to, :] = own.astype(jnp.bfloat16)
+            return carry
+
+        lax.fori_loop(0, groups, body, 0)
+        far_copy(index).start()
+
+    def finish_sum(index):
+        far_copy(index).wait_recv()
+
+        def body(group, squares):
+            to = pl.ds(pl.multiple_of(group * 2 * SUB, 2 * SUB), 2 * SUB)
+            own = keep[index][0, to, :].astype(jnp.float32) + near[index][0, to, :].astype(jnp.float32)
+            own = own + far[index][to, :].astype(jnp.float32)
+            keep[index][0, to, :] = own.astype(jnp.bfloat16)
+            return squares + own * own
+
+        start = jnp.zeros((2 * SUB, cuts[index]), jnp.float32)
+        squares = lax.fori_loop(0, groups, body, start)
+        return (
+            jnp.sum(squares[:SUB], axis=0, keepdims=True),
+            jnp.sum(squares[SUB:], axis=0, keepdims=True),
+        )
+
+    def send_map(index, weights, squares):
+        product = lax.dot_general(
+            unit_rows[...], weights, (((0,), (0,)), ((), ())), preferred_element_type=jnp.float32
+        ).astype(jnp.bfloat16)
+        share = g_send[index].shape[1]
+        for goal in range(n):
+            g_send[index][goal] = product[goal * share:(goal + 1) * share]
+        q_send[index][0] = squares[0]
+        q_send[index][1] = squares[1]
+
+        def act(step):
+            for copy in map_copies(index, step):
+                copy.start()
+
+        each_peer(act)
+
+    def finish_map(index):
+        def act(step):
+            for copy in map_copies(index, step):
+                copy.wait_recv()
+
+        each_peer(act)
+        product = g_send[index][me].astype(jnp.float32)
+        squares = q_send[index][(me * 2) // n]
+        for step in range(1, n):
+            product = product + g_recv[index][step].astype(jnp.float32)
+            squares = squares + q_recv[index][step]
+        scaled = product * (1.0 / (EPS + jnp.sqrt(squares)))
+        k_out[index][me] = scaled.astype(jnp.bfloat16)
+        each_peer(lambda step: map_spread(index, step).start())
+
+    def unit_in_rows(values):
+        lane = lax.broadcasted_iota(jnp.int32, values.shape, 1)
+        left = jnp.where(lane < LANES // 2, values, 0.0)
+        norm = jnp.sqrt(jnp.sum(left * left, axis=1, keepdims=True))
+        return left / (EPS + norm)
+
+    def start_aux():
+        squares = finish_sum(0)
+        own = keep[0][0, :, 0:LANES]
+        aux_all[me] = own
+        each_peer(lambda step: aux_copy(step).start())
+        unit = unit_in_rows(own.astype(jnp.float32))
+        unit = unit + pltpu.roll(unit, LANES // 2, 1)
+        row = lax.broadcasted_iota(jnp.int32, unit.shape, 0)
+        lane = lax.broadcasted_iota(jnp.int32, unit.shape, 1)
+        same = lax.rem(row, 2 * SUB) // SUB == lane // (LANES // 2)
+        unit_rows[...] = jnp.where(same, unit, 0.0).astype(jnp.bfloat16)
+        rest = keep[0][0, :, LANES:]
+        proj_width = proj_w.shape[1] - LANES
+        proj_w[:, proj_width:] = jnp.where(lane < LANES // 2, rest, jnp.zeros_like(rest))
+        first = lax.broadcasted_iota(jnp.int32, (1, LANES), 1) < LANES // 2
+        for profile in range(2):
+            proj_sq[profile, :, proj_width:] = jnp.where(first, squares[profile][:, LANES:], 0.0)
+        send_map(0, rest, [square[:, LANES:] for square in squares])
+
+    def start_proj(index, offset):
+        squares = finish_sum(index)
+        proj_w[:, offset:offset + cuts[index]] = keep[index][0]
+        for profile in range(2):
+            proj_sq[profile, :, offset:offset + cuts[index]] = squares[profile]
+
+    def out_maps():
+        each_peer(lambda step: aux_copy(step).wait_recv())
+        each_peer(lambda step: sq_copy(step).wait_recv())
+        sums = proj_sq[...]
+        for step in range(1, n):
+            sums = sums + proj_sq_in[step]
+        inverse = 1.0 / (EPS + jnp.sqrt(sums))
+        values = aux_all[...].astype(jnp.float32).reshape(n * groups, 2 * SUB, LANES)
+        results = []
+        depth = n * real
+        for profile in range(2):
+            own = values[:, profile * SUB:(profile + 1) * SUB].reshape(n * groups * SUB, LANES)
+            if real < groups * SUB:
+                starts = range(0, n * groups * SUB, groups * SUB)
+                own = jnp.concatenate([own[start:start + real] for start in starts], axis=0)
+            norm = jnp.sqrt(jnp.sum(own * own, axis=0, keepdims=True))
+            unit_out = (own / (EPS + norm)).astype(jnp.bfloat16)
+            unit_in = unit_in_rows(own).astype(jnp.bfloat16)
+            skip_out[profile] = lax.dot_general(
+                unit_in, unit_out, (((0,), (0,)), ((), ())), preferred_element_type=jnp.float32
+            )
+            spare = jnp.zeros((proj_w.shape[1] - depth, LANES), jnp.bfloat16)
+            tall = jnp.concatenate([unit_out, spare], axis=0)
+            weights = (proj_w[...].astype(jnp.float32) * inverse[profile]).astype(jnp.bfloat16)
+            results.append(jnp.dot(weights, tall, preferred_element_type=jnp.float32))
+        row = lax.broadcasted_iota(jnp.int32, results[0].shape, 0)
+        chosen = jnp.where(lax.rem(row, 2 * SUB) < SUB, results[0], results[1])
+        m_out[me] = chosen.astype(jnp.bfloat16)
+        each_peer(lambda step: m_copy(step).start())
+
+    fetch(0).start()
+    for index in range(total):
+        if index + 1 < total:
+            fetch(index + 1).start()
+        fetch(index).wait()
+        contract(index)
+        if index == 0:
+            pl.semaphore_wait(barrier, n + 1)
+        near_copy(index).start()
+        if index >= 1:
+            pass_on(index - 1)
+    pass_on(total - 1)
+
+    start_aux()
+    offset = 0
+    for index in range(1, proj_count + 1):
+        start_proj(index, offset)
+        offset += cuts[index]
+    each_peer(lambda step: sq_copy(step).start())
+    finish_map(0)
+    for index in range(1, maps):
+        chunk = index + proj_count
+        squares = finish_sum(chunk)
+        send_map(index, keep[chunk][0], squares)
+        if index == 1:
+            out_maps()
+        if index >= 2:
+            finish_map(index - 1)
+    finish_map(maps - 1)
+
+    for index in range(maps):
+        each_peer(lambda step: map_spread(index, step).wait_recv())
+    each_peer(lambda step: m_copy(step).wait_recv())
+    for index in range(total):
+        near_copy(index).wait_send()
+        far_copy(index).wait_send()
+
+    def drain(step):
+        for index in range(maps):
+            for copy in map_copies(index, step):
+                copy.wait_send()
+            map_spread(index, step).wait_send()
+        aux_copy(step).wait_send()
+        sq_copy(step).wait_send()
+        m_copy(step).wait_send()
+
+    each_peer(drain)
+
+
+def exchange_call(coeffs, aux, proj, qkv, n, real, main_proj, main_qkv):
+    snaps, rows, _ = aux.shape
+    groups = rows // SUB
+    proj_cuts = cut(main_proj, 2)
+    cuts = [aux.shape[2]] + proj_cuts + cut(main_qkv, 5)
+    total = len(cuts)
+    map_cuts = [LANES] + cuts[1 + len(proj_cuts):]
+    maps = len(map_cuts)
+    both = 2 * rows
+    share = LANES // n
+    proj_wide = main_proj + LANES
+    kind, wide = jnp.bfloat16, jnp.float32
+    shapes = [jax.ShapeDtypeStruct((n, share, width), kind) for width in map_cuts]
+    shapes += [
+        jax.ShapeDtypeStruct((n, both, LANES), kind),
+        jax.ShapeDtypeStruct((2, LANES, LANES), wide),
+    ]
+    scratch = [pltpu.VMEM((2, snaps, rows, max(cuts)), wide)]
+    for lead in ((2,), (2,), (2,), (), ()):
+        scratch += [pltpu.VMEM(lead + (both, width), kind) for width in cuts]
+    scratch += [pltpu.VMEM((n, share, width), kind) for width in map_cuts]
+    scratch += [pltpu.VMEM((n, share, width), kind) for width in map_cuts]
+    scratch += [pltpu.VMEM((2, 1, width), wide) for width in map_cuts]
+    scratch += [pltpu.VMEM((n, 1, width), wide) for width in map_cuts]
+    scratch += [
+        pltpu.VMEM((n, both, LANES), kind),
+        pltpu.VMEM((both, proj_wide), kind),
+        pltpu.VMEM((2, 1, proj_wide), wide),
+        pltpu.VMEM((n, 2, 1, proj_wide), wide),
+        pltpu.VMEM((both, LANES), kind),
+        pltpu.SemaphoreType.DMA((2,)),
+        pltpu.SemaphoreType.DMA((2, total)),
+        pltpu.SemaphoreType.DMA((2, total)),
+        pltpu.SemaphoreType.DMA((2, maps, 3, n)),
+        pltpu.SemaphoreType.DMA((2, n)),
+        pltpu.SemaphoreType.DMA((2, n)),
+        pltpu.SemaphoreType.DMA((2, n)),
+    ]
+    hbm = pl.BlockSpec(memory_space=pl.ANY)
+    return pl.pallas_call(
+        functools.partial(exchange_kernel, tuple(cuts), len(proj_cuts), n, groups, real),
+        out_shape=shapes,
+        in_specs=[pl.BlockSpec(memory_space=pltpu.SMEM), hbm, hbm, hbm],
+        out_specs=[pl.BlockSpec(memory_space=pltpu.VMEM)] * len(shapes),
+        scratch_shapes=scratch,
+        compiler_params=pltpu.CompilerParams(
+            collective_id=0, has_side_effects=True, vmem_limit_bytes=60 * 2**20
+        ),
+    )(coeffs, aux, proj, qkv)
 
 
 def shards(snap_in, snap_qkv, snap_proj, snap_out, coeffs, latent, levels):
     owned = PROF // lax.axis_size("snap")
-    prof_in = reduced(coeffs, snap_in)
-    prof_out = reduced(coeffs, snap_out)
-    prof_proj = reduced(coeffs, snap_proj)
-    prof_qkv = reduced(coeffs, snap_qkv)
-    unit_in = (prof_in * inverse_norms(squares(prof_in))[:, None, :]).astype(jnp.bfloat16)
-    full_out = lax.all_gather(prof_out, "param", axis=1, tiled=True)
-    unit_out = full_out * inverse_norms(squares(full_out))[:, None, :]
-    part_map = rows_product(unit_in, prof_qkv)
-    part_skip = jnp.einsum(
-        "pfr,prc->pfc", unit_in.astype(jnp.float32), prof_out, precision=lax.Precision.HIGHEST
+    n = lax.axis_size("param")
+    snap = lax.axis_index("snap")
+    width = snap_proj.shape[2]
+    rows = snap_qkv.shape[1]
+    main_proj = width // LANES * LANES
+    main_qkv = snap_qkv.shape[2] // LANES * LANES
+    aux = jnp.concatenate(
+        [snap_in.transpose(0, 2, 1), snap_out, snap_proj[:, :, main_proj:], snap_qkv[:, :, main_qkv:]],
+        axis=2,
     )
-    sums_qkv, sums_proj, qkv_map, skip_map = lax.psum(
-        (squares(prof_qkv), squares(prof_proj), part_map, part_skip), "param"
-    )
-    qkv_map = (qkv_map * inverse_norms(sums_qkv)[:, None, :]).astype(jnp.bfloat16)
-    skip_map = skip_map * inverse_norms(squares(full_out))[:, None, :]
-    scaled_out = (unit_out * inverse_norms(sums_proj)[:, :, None]).astype(jnp.bfloat16)
-    own_rows = jnp.einsum(
-        "prc,pcf->prf", prof_proj.astype(jnp.bfloat16), scaled_out, preferred_element_type=jnp.float32
-    ).astype(jnp.bfloat16)
-    out_map = lax.all_gather(own_rows, "param", axis=1, tiled=True)
+    main = [snap_proj, snap_qkv]
+    spare = -rows % SUB
+    if spare:
+        aux, *main = [jnp.pad(x, ((0, 0), (0, spare), (0, 0))) for x in [aux] + main]
+    order = jnp.stack([snap, (snap + 2) % 4, snap + 1 - 2 * (snap % 2), (snap + 3 - 2 * (snap % 2)) % 4])
+    columns = jnp.take(coeffs.reshape(-1, 4, owned), order, axis=1).reshape(coeffs.shape)
+    *maps, out_map, skip_map = exchange_call(columns, aux, main[0], main[1], n, rows, main_proj, main_qkv)
+    maps = [part.reshape(owned, -1, part.shape[2]) for part in maps]
+    half = LANES // 2
+    qkv_map = jnp.concatenate(maps[1:] + [maps[0][:, :, half:]], axis=2)
+    out_map = out_map.reshape(n, -1, owned, SUB, LANES)[..., half:]
+    out_map = out_map.transpose(2, 0, 1, 3, 4).reshape(owned, n, -1, half)[:, :, :rows]
+    out_map = out_map.reshape(owned, n * rows, half)
+    skip_map = skip_map[:, :half, half:]
     tokens, c_skip, c_out = prepare(latent, levels)
     results = []
     for profile in range(owned):

time: 405 us -> 154 us (0.38)
  waiting for transfers between devices: 198 us -> 0 us
  Pallas kernels: 0 us -> 117 us
  blocking collectives: 72.1 us -> 0 us
  matrix products: 65.5 us -> 8.23 us
  local copies, waits for them, and re-layouts: 38.5 us -> 21.1 us
  between operations: 14.7 us -> 1.19 us
  other arithmetic: 15.3 us -> 5.2 us
    psum x2 -> x0, waiting for transfers between devices: 138 us -> none  [shards(): lax.psum((squares(prof_qkv), squares(prof_proj), part_map, part_skip), 'p...]
    pallas_call x0 -> x1, Pallas kernels: none -> 117 us  [exchange_call(): pl.pallas_call(functools.partial(exchange_kernel, tuple(cuts), len(proj_c...]
    all_gather x2 -> x0, blocking collectives: 72.1 us -> none  [the longest x1 37.4 us: shards(): full_out = lax.all_gather(prof_out, 'param', axis=1, tiled=True)]
    reduce_scatter x4 -> x0, waiting for transfers between devices: 60.7 us -> none  [reduced(): lax.psum_scatter(part, 'snap', scatter_dimension=0, tiled=True)]
    dot_general x7 -> x0, matrix products: 56.5 us -> none  [the longest x4 51 us: contract(): jnp.einsum('sp,sij->pij', coeffs, snaps, precision=lax.Precision.HIGHEST)]
    convert_element_type x6 -> x0, local copies, waits for them, and re-layouts: 21.2 us -> none  [the longest x4 20.1 us: reduced(): part = contract(coeffs, snaps).astype(jnp.bfloat16)]
    reduce_sum x4 -> x0, other arithmetic: 7.82 us -> none  [squares(): return jnp.sum(weights * weights, axis=1)]
    unnamed x23 -> x17, local copies, waits for them, and re-layouts: 3.24 us -> 8.3 us
  transfers between devices with their start and end apart: 6 -> 0, of which waited for: 3 -> 0; matrix products, arithmetic and copies ran while one was open for 22% -> 0% of each run, Pallas kernels for 0% -> 0%
where the time goes in v2:
time: 154 us; the launch traced here: 153 us
  Pallas kernels  117 us (76%)
  local copies, waits for them, and re-layouts  21.1 us (14%)
  matrix products  8.23 us (5%)
  other arithmetic  5.2 us (3%)
    pallas_call x1, Pallas kernels, exchange_call(): pl.pallas_call(functools.partial(exchange_kernel, tuple(cuts), len(proj_c...  117 us
    unnamed x17, local copies, waits for them, and re-layouts  8.3 us
    mul x6, local copies, waits for them, and re-layouts, finish(): return c_skip[:, None, None] * latent + c_out[:, None, None] * image  6.49 us
    convert_element_type x4, local copies, waits for them, and re-layouts, prepare(): to_tokens(c_in[:, None, None] * latent).reshape(count * 256, 64)  3.51 us

profile of v2, /device:TPU:0, one launch (start us, length us, event | category | flops | bytes accessed | tf_op | source)
XLA Modules:
  0.0 153.2 jit_solution(7508086677742741069)
XLA Ops:
  0.3 0.9 copy.19
  1.2 0.6 gather_fusion
  1.8 0.6 broadcast_select_fusion.coeffs
  2.4 1.3 copy.21
  3.7 1.3 copy.22
  5.1 1.7 %pad_maximum_fusion.aux = f32[8,168,256]{2,1,0:T(8,128)} fusion(f32[8,168,64]{2,1,0:T(8,128)S(1)} %slice-done, f32[8,168,64]{2,1,0:T(8,128)S(1)} %slice-done.1, f32[8,168,64]{2,1,0:T(8,128)S(1)} %copy.22, f32[8,168,64]{2,1,0:T(8,128)S(1)} %bitcast.129), kind=kLoop, calls=%fused_computation.13 | loop fusion | flops 1032192 | bytes 2752512 | tf_op jit(solution)/shard_map/concatenate | solution.py:455
  6.8 117.5 %shard_map.73 = (bf16[8,16,128]{2,1,0:T(8,128)(2,1)}, bf16[8,16,896]{2,1,0:T(8,128)(2,1)}, bf16[8,16,768]{2,1,0:T(8,128)(2,1)}, bf16[8,16,768]{2,1,0:T(8,128)(2,...) custom-call(f32[8,8]{1,0:T(8,128)} %broadcast_select_fusion.coeffs, ...), custom_call_target="tpu_custom_call" | custom-call | tf_op jit(solution)/shard_map/pallas_call | solution.py:435
  124.2 1.0 bitcast_dynamic-update-slice_fusion
  125.2 0.9 bitcast_dynamic-update-slice_fusion.4
  126.2 0.9 bitcast_dynamic-update-slice_fusion.3
  127.1 0.9 bitcast_dynamic-update-slice_fusion.2
  128.1 0.9 bitcast_dynamic-update-slice_fusion.1
  129.0 0.8 slice_dynamic-update-slice_fusion
  130.8 1.2 convert_element_type.70
  132.0 2.0 %copy.18 = bf16[1,16,16,4,4,4]{2,1,5,4,3,0:T(8,128)(2,1)S(1)} copy(bf16[1,16,16,4,4,4]{3,1,5,4,2,0:T(8,128)(2,1)S(1)} %bitcast.128) | data formatting | bytes 65536 | tf_op jit(solution)/shard_map/convert_element_type | solution.py:70
  134.2 0.8 fusion.12
  135.0 0.6 multiply_reduce_fusion
  135.6 0.6 divide_convert_fusion.2
  136.2 1.2 fusion.1
  137.4 1.1 fusion.4
  138.5 0.3 convolution_multiply_fusion.1
  139.7 2.0 %copy.26 = f32[1,16,16,4,4,4]{3,1,5,4,2,0:T(8,128)S(1)} copy(f32[1,16,16,4,4,4]{2,1,5,4,3,0:T(8,128)S(1)} %mul.157) | data formatting | bytes 131072 | tf_op jit(solution)/shard_map/mul | solution.py:77
  141.8 1.0 mul.159
  142.8 1.8 %fusion.13 = f32[256,4032]{0,1:T(8,128)S(1)} fusion(bf16[256,64]{0,1:T(8,128)(2,1)S(1)} %convert_element_type.72, bf16[2,64,4032]{2,1,0:T(8,128)(2,1)} %copy-done), kind=kOutput, calls=%fused_computation.36 | convolution fusion | flops 132120576 | bytes 4685824 | tf_op jit(solution)/shard_map/dot_general | solution.py:51
  144.6 0.6 multiply_reduce_fusion.1
  145.3 0.8 divide_convert_fusion.3
  146.1 1.2 fusion
  147.2 1.1 fusion.5
  148.3 0.3 convolution_multiply_fusion.3
  149.1 2.0 %copy.24 = f32[1,16,16,4,4,4]{3,1,5,4,2,0:T(8,128)S(1)} copy(f32[1,16,16,4,4,4]{2,1,5,4,3,0:T(8,128)S(1)} %mul.149) | data formatting | bytes 131072 | tf_op jit(solution)/shard_map/mul | solution.py:77
  151.2 1.0 mul.151
  152.4 0.8 copy.27
  (32 shorter events, 2.3 us)
Async XLA Ops:
  0.0 5.1 %slice-start.1 = ((f32[8,168,1344]{2,1,0:T(8,128)}), f32[8,168,64]{2,1,0:T(8,128)S(1)}, s32[]{:S(2)}) async-start(f32[8,168,1344]{2,1,0:T(8,128)} %proj.1), calls=%async_computation.1 | async-start | bytes 1376256 | tf_op jit(solution)/shard_map/slice | solution.py:456
  0.0 5.1 %slice-start = ((f32[8,168,4032]{2,1,0:T(8,128)}), f32[8,168,64]{2,1,0:T(8,128)S(1)}, s32[]{:S(2)}) async-start(f32[8,168,4032]{2,1,0:T(8,128)} %qkv.1), calls=%async_computation | async-start | bytes 1376256 | tf_op jit(solution)/shard_map/slice | solution.py:456
  6.8 123.9 %copy-start.2 = (f32[1,64,256]{2,1,0:T(8,128)S(1)}, f32[1,64,256]{2,1,0:T(8,128)}, u32[]{:S(2)}) copy-start(f32[1,64,256]{2,1,0:T(8,128)} %param.12) | copy-start | bytes 196612
  129.9 5.7 %copy-start = (bf16[2,64,4032]{2,1,0:T(8,128)(2,1)}, bf16[2,64,4032]{2,1,0:T(8,128)(2,1)S(1)}, u32[]{:S(2)}) copy-start(bf16[2,64,4032]{2,1,0:T(8,128)(2,1)S(1)} %slice_dynamic-update-slice_fusion) | copy-start | bytes 3096580
  137.4 1.1 copy-start.3
  137.4 1.4 copy-start.1

commit v3 on v2

--- a/solution.py
+++ b/solution.py
@@ -88,13 +88,48 @@
     return [size * LANES for size in sizes if size]
 
 
+def head_plan(pairs):
+    sizes = cut(pairs * LANES, 5)
+    sizes = [size // LANES for size in sizes]
+    if len(sizes) > 2 and sizes[-1] > 1:
+        sizes[0] += 1
+        sizes[-1] -= 1
+    plan = []
+    first = 0
+    for size in sizes:
+        last = first + size
+        key_first = first + 1 if first else 0
+        plan.append(
+            (
+                (first, last),
+                (pairs + key_first, pairs + last + 1),
+                (2 * pairs + 1 + first, 2 * pairs + 1 + last),
+            )
+        )
+        first = last
+    return tuple(plan)
+
+
+def tile_places(plan):
+    places = {}
+    for index, parts in enumerate(plan):
+        lane = 0
+        for first, last in parts:
+            for tile in range(first, last):
+                places[tile] = (index + 1, lane)
+                lane += LANES
+    places[len(places)] = (0, 0)
+    return places
+
+
 def exchange_kernel(
-    cuts, proj_count, n, groups, real,
-    coeffs, aux, proj, qkv,
+    plan, cuts, proj_count, n, groups, real, fused,
+    coeffs, aux, proj, qkv, tokens,
     *refs,
 ):
     total = len(cuts)
     maps = total - proj_count
+    places = tile_places(plan)
     pos = 0
 
     def take(count):
@@ -103,11 +138,11 @@
         return refs[pos - count:pos]
 
     k_out = take(maps)
-    (m_out, skip_out) = take(2)
+    (m_out, skip_out, feature) = take(3)
     (feed,) = take(1)
     away, keep, near, over, far = (take(total) for _ in range(5))
     g_send, g_recv, q_send, q_recv = (take(maps) for _ in range(4))
-    (aux_all, proj_w, proj_sq, proj_sq_in, unit_rows) = take(5)
+    (aux_all, proj_w, proj_sq, proj_sq_in, unit_rows, out_rows) = take(6)
     (feed_sem, near_sems, far_sems, map_sems, aux_sems, sq_sems, m_sems) = take(7)
 
     rows = groups * 2 * SUB
@@ -135,26 +170,27 @@
 
     lax.fori_loop(1, n, greet, 0)
 
-    sources = []
-    offset = 0
-    sources.append((aux, 0))
-    for index in range(1, total):
-        if index <= proj_count:
-            sources.append((proj, offset))
-        else:
-            sources.append((qkv, offset))
-        offset += cuts[index]
-        if index == proj_count:
-            offset = 0
-
-    def fetch(index):
-        source, start = sources[index]
+    starts = [[(0, cuts[0])]]
+    for index in range(proj_count):
+        starts.append([(sum(cuts[1:1 + index]), cuts[1 + index])])
+    for parts in plan:
+        starts.append([(first * LANES, (last - first) * LANES) for first, last in parts])
+    sources = [aux] + [proj] * proj_count + [qkv] * len(plan)
+
+    def fetches(index):
         slot = index % 2
-        return pltpu.make_async_copy(
-            source.at[:, :, start:start + cuts[index]],
-            feed.at[slot, :, :, 0:cuts[index]],
-            feed_sem.at[slot],
-        )
+        copies = []
+        at = 0
+        for which, (start, width) in enumerate(starts[index]):
+            copies.append(
+                pltpu.make_async_copy(
+                    sources[index].at[:, :, start:start + width],
+                    feed.at[slot, :, :, at:at + width],
+                    feed_sem.at[slot, which],
+                )
+            )
+            at += width
+        return copies
 
     def remote(source, target, sems, at, device):
         return pltpu.make_async_remote_copy(
@@ -196,6 +232,8 @@
 
     def m_copy(step):
         return remote(m_out.at[me], m_out.at[me], m_sems, (step,), peer(step))
+
+    pairs = (snap, across, sibling, lax.rem(sibling + 2, 4))
 
     def contract(index):
         width = cuts[index]
@@ -209,7 +247,7 @@
                 snaps = [feed[slot, s, at, lanes] for s in range(feed.shape[1])]
                 for pair in range(4):
                     both = []
-                    for column in (2 * pair, 2 * pair + 1):
+                    for column in (2 * pairs[pair], 2 * pairs[pair] + 1):
                         value = coeffs[0, column] * snaps[0]
                         for s in range(1, len(snaps)):
                             value = value + coeffs[s, column] * snaps[s]
@@ -344,11 +382,14 @@
         m_out[me] = chosen.astype(jnp.bfloat16)
         each_peer(lambda step: m_copy(step).start())
 
-    fetch(0).start()
+    for copy in fetches(0):
+        copy.start()
     for index in range(total):
         if index + 1 < total:
-            fetch(index + 1).start()
-        fetch(index).wait()
+            for copy in fetches(index + 1):
+                copy.start()
+        for copy in fetches(index):
+            copy.wait()
         contract(index)
         if index == 0:
             pl.semaphore_wait(barrier, n + 1)
@@ -364,19 +405,90 @@
         offset += cuts[index]
     each_peer(lambda step: sq_copy(step).start())
     finish_map(0)
+
+    def arrived(index):
+        each_peer(lambda step: map_spread(index, step).wait_recv())
+
+    def product_of(index, lane, profile):
+        half = n // 2
+        weights = k_out[index][pl.ds(profile * half, half), :, lane:lane + LANES]
+        return jnp.dot(
+            tokens[...], weights.reshape(LANES // 2, LANES), preferred_element_type=jnp.float32
+        )
+
+    def start_attention():
+        each_peer(lambda step: m_copy(step).wait_recv())
+        values = m_out[...].astype(jnp.float32).reshape(n * groups, 2 * SUB, LANES)
+        for profile in range(2):
+            own = values[:, profile * SUB:(profile + 1) * SUB].reshape(n * real, LANES)
+            out_rows[profile] = own.astype(jnp.bfloat16)
+            skip = jnp.dot(
+                tokens[...].astype(jnp.float32), skip_out[profile, 0:LANES // 2],
+                preferred_element_type=jnp.float32, precision=lax.Precision.HIGHEST,
+            )
+            feature[profile] = 0.7 * skip
+
+    def attention(which):
+        first, last = plan[which][0]
+        heads = list(range(2 * first, 2 * last))
+        count = proj.shape[2] // HEAD_DIM
+        if which == len(plan) - 1:
+            heads.append(count - 1)
+
+        def body(profile, carry):
+            found = {}
+
+            def unit(column):
+                tile, lane = column // LANES, column % LANES
+                if tile not in found:
+                    found[tile] = product_of(*places[tile], profile)
+                if tile == len(places) - 1:
+                    lane = LANES // 2
+                own = found[tile][:, lane:lane + HEAD_DIM]
+                scale = jnp.sqrt(jnp.mean(own * own, axis=1, keepdims=True))
+                return (own * (1.0 / (EPS + scale))).astype(jnp.bfloat16)
+
+            added = jnp.zeros(feature.shape[1:], jnp.float32)
+            for head in heads:
+                query, keys, values = (
+                    unit((part * count + head) * HEAD_DIM) for part in range(3)
+                )
+                scores = lax.dot_general(
+                    query, keys, (((1,), (1,)), ((), ())), preferred_element_type=jnp.float32
+                )
+                expo = jnp.exp(scores * (1.0 / HEAD_DIM**0.5))
+                weights = expo * (1.0 / jnp.sum(expo, axis=1, keepdims=True))
+                mixed = jnp.dot(
+                    weights.astype(jnp.bfloat16), values, preferred_element_type=jnp.float32
+                ).astype(jnp.bfloat16)
+                rows_of = out_rows[profile, head * HEAD_DIM:(head + 1) * HEAD_DIM, :]
+                added = added + jnp.dot(mixed, rows_of, preferred_element_type=jnp.float32)
+            feature[profile] = feature[profile] + 0.3 * added
+            return carry
+
+        lax.fori_loop(0, 2, body, 0)
+
     for index in range(1, maps):
         chunk = index + proj_count
         squares = finish_sum(chunk)
         send_map(index, keep[chunk][0], squares)
         if index == 1:
             out_maps()
-        if index >= 2:
-            finish_map(index - 1)
-    finish_map(maps - 1)
-
-    for index in range(maps):
-        each_peer(lambda step: map_spread(index, step).wait_recv())
-    each_peer(lambda step: m_copy(step).wait_recv())
+            arrived(0)
+        elif fused:
+            if index == 2:
+                start_attention()
+            arrived(index - 1)
+            attention(index - 2)
+        finish_map(index)
+    arrived(maps - 1)
+    if fused:
+        attention(maps - 2)
+    else:
+        for index in range(1, maps - 1):
+            arrived(index)
+        each_peer(lambda step: m_copy(step).wait_recv())
+        feature[...] = jnp.zeros(feature.shape, feature.dtype)
     for index in range(total):
         near_copy(index).wait_send()
         far_copy(index).wait_send()
@@ -393,11 +505,12 @@
     each_peer(drain)
 
 
-def exchange_call(coeffs, aux, proj, qkv, n, real, main_proj, main_qkv):
+def exchange_call(coeffs, aux, proj, qkv, tokens, n, real, main_proj, plan, fused):
     snaps, rows, _ = aux.shape
     groups = rows // SUB
     proj_cuts = cut(main_proj, 2)
-    cuts = [aux.shape[2]] + proj_cuts + cut(main_qkv, 5)
+    cuts = [aux.shape[2]] + proj_cuts
+    cuts += [sum(last - first for first, last in parts) * LANES for parts in plan]
     total = len(cuts)
     map_cuts = [LANES] + cuts[1 + len(proj_cuts):]
     maps = len(map_cuts)
@@ -409,6 +522,7 @@
     shapes += [
         jax.ShapeDtypeStruct((n, both, LANES), kind),
         jax.ShapeDtypeStruct((2, LANES, LANES), wide),
+        jax.ShapeDtypeStruct((2, tokens.shape[0], LANES), wide),
     ]
     scratch = [pltpu.VMEM((2, snaps, rows, max(cuts)), wide)]
     for lead in ((2,), (2,), (2,), (), ()):
@@ -423,7 +537,8 @@
         pltpu.VMEM((2, 1, proj_wide), wide),
         pltpu.VMEM((n, 2, 1, proj_wide), wide),
         pltpu.VMEM((both, LANES), kind),
-        pltpu.SemaphoreType.DMA((2,)),
+        pltpu.VMEM((2, n * real, LANES), kind),
+        pltpu.SemaphoreType.DMA((2, 3)),
         pltpu.SemaphoreType.DMA((2, total)),
         pltpu.SemaphoreType.DMA((2, total)),
         pltpu.SemaphoreType.DMA((2, maps, 3, n)),
@@ -433,21 +548,25 @@
     ]
     hbm = pl.BlockSpec(memory_space=pl.ANY)
     return pl.pallas_call(
-        functools.partial(exchange_kernel, tuple(cuts), len(proj_cuts), n, groups, real),
+        functools.partial(
+            exchange_kernel, plan, tuple(cuts), len(proj_cuts), n, groups, real, fused
+        ),
         out_shape=shapes,
-        in_specs=[pl.BlockSpec(memory_space=pltpu.SMEM), hbm, hbm, hbm],
+        in_specs=[
+            pl.BlockSpec(memory_space=pltpu.SMEM), hbm, hbm, hbm,
+            pl.BlockSpec(memory_space=pltpu.VMEM),
+        ],
         out_specs=[pl.BlockSpec(memory_space=pltpu.VMEM)] * len(shapes),
         scratch_shapes=scratch,
         compiler_params=pltpu.CompilerParams(
             collective_id=0, has_side_effects=True, vmem_limit_bytes=60 * 2**20
         ),
-    )(coeffs, aux, proj, qkv)
+    )(coeffs, aux, proj, qkv, tokens)
 
 
 def shards(snap_in, snap_qkv, snap_proj, snap_out, coeffs, latent, levels):
     owned = PROF // lax.axis_size("snap")
     n = lax.axis_size("param")
-    snap = lax.axis_index("snap")
     width = snap_proj.shape[2]
     rows = snap_qkv.shape[1]
     main_proj = width // LANES * LANES
@@ -460,17 +579,28 @@
     spare = -rows % SUB
     if spare:
         aux, *main = [jnp.pad(x, ((0, 0), (0, spare), (0, 0))) for x in [aux] + main]
-    order = jnp.stack([snap, (snap + 2) % 4, snap + 1 - 2 * (snap % 2), (snap + 3 - 2 * (snap % 2)) % 4])
-    columns = jnp.take(coeffs.reshape(-1, 4, owned), order, axis=1).reshape(coeffs.shape)
-    *maps, out_map, skip_map = exchange_call(columns, aux, main[0], main[1], n, rows, main_proj, main_qkv)
+    plan = head_plan(width // LANES)
+    share = owned * snap_in.shape[1] // n
+    fused = rows % SUB == 0 and share % (2 * SUB) == 0 and latent.shape[0] == 1
+    tokens, c_skip, c_out = prepare(latent, levels)
+    *maps, out_map, skip_map, feature = exchange_call(
+        coeffs, aux, main[0], main[1], tokens, n, rows, main_proj, plan, fused
+    )
+    half = LANES // 2
+    if fused:
+        feature = feature[:, :, half:] / jnp.sqrt(0.58)
+        return jax.vmap(lambda value: finish(value, latent, c_skip, c_out))(feature)
     maps = [part.reshape(owned, -1, part.shape[2]) for part in maps]
-    half = LANES // 2
-    qkv_map = jnp.concatenate(maps[1:] + [maps[0][:, :, half:]], axis=2)
+    places = tile_places(plan)
+    tiles = []
+    for tile in range(len(places) - 1):
+        index, lane = places[tile]
+        tiles.append(maps[index][:, :, lane:lane + LANES])
+    qkv_map = jnp.concatenate(tiles + [maps[0][:, :, half:]], axis=2)
     out_map = out_map.reshape(n, -1, owned, SUB, LANES)[..., half:]
     out_map = out_map.transpose(2, 0, 1, 3, 4).reshape(owned, n, -1, half)[:, :, :rows]
     out_map = out_map.reshape(owned, n * rows, half)
     skip_map = skip_map[:, :half, half:]
-    tokens, c_skip, c_out = prepare(latent, levels)
     results = []
     for profile in range(owned):
         feature = attend(tokens, qkv_map[profile], out_map[profile], skip_map[profile])

time: 154 us -> 172 us (1.12)
  Pallas kernels: 117 us -> 151 us
  matrix products: 8.23 us -> 0 us
  local copies, waits for them, and re-layouts: 21.1 us -> 16 us
    pallas_call x1, Pallas kernels: 117 us -> 151 us  [exchange_call(): pl.pallas_call(functools.partial(exchange_kernel, plan, tuple(cuts), len(...]
    dot_general x10 -> x0, matrix products: 8.23 us -> none  [the longest x2 2.54 us: attend(): qkv = jnp.dot(tokens, mixed_qkv, preferred_element_type=jnp.float32)]
    unnamed x17 -> x6, local copies, waits for them, and re-layouts: 8.3 us -> 0.54 us
    mul x6 -> x4, local copies, waits for them, and re-layouts: 6.49 us -> 9 us  [finish(): return c_skip[:, None, None] * latent + c_out[:, None, None] * image]
    convert_element_type x4 -> x5, local copies, waits for them, and re-layouts: 3.51 us -> 4.24 us  [prepare(): to_tokens(c_in[:, None, None] * latent).reshape(count * 256, 64)]
where the time goes in v3:
time: 172 us; the launch traced here: 171 us
  Pallas kernels  151 us (88%)
  local copies, waits for them, and re-layouts  16 us (9%)
  other arithmetic  3.67 us (2%)
    pallas_call x1, Pallas kernels, exchange_call(): pl.pallas_call(functools.partial(exchange_kernel, plan, tuple(cuts), len(...  151 us
    mul x4, local copies, waits for them, and re-layouts, finish(): return c_skip[:, None, None] * latent + c_out[:, None, None] * image  9 us
    convert_element_type x5, local copies, waits for them, and re-layouts, prepare(): to_tokens(c_in[:, None, None] * latent).reshape(count * 256, 64)  4.24 us

profile of v3, /device:TPU:0, one launch (start us, length us, event | category | flops | bytes accessed | tf_op | source)
XLA Modules:
  0.0 171.4 jit_solution(7413459164484450677)
XLA Ops:
  0.8 0.9 multiply_bitcast_fusion
  1.7 0.1 copy.24
  1.8 0.0 copy-start
  1.8 1.2 convert_element_type.14
  3.0 0.0 copy-start.1
  3.0 2.0 %copy.25 = bf16[1,16,16,4,4,4]{2,1,5,4,3,0:T(8,128)(2,1)S(1)} copy(bf16[1,16,16,4,4,4]{3,1,5,4,2,0:T(8,128)(2,1)S(1)} %bitcast.21) | data formatting | bytes 65536 | tf_op jit(solution)/shard_map/convert_element_type | solution.py:70
  5.0 0.2 convert_element_type.16
  5.2 0.7 copy.26.tokens
  6.0 0.0 copy-done
  6.0 0.3 copy.22
  6.2 0.0 copy-done.1
  6.2 0.3 copy.23
  6.5 0.0 slice-start
  6.5 0.0 slice-start.1
  6.5 1.1 slice-done
  7.6 0.2 slice-done.1
  7.8 1.7 pad_maximum_fusion.aux
  9.5 150.8 %shard_map.73 = (bf16[8,16,128]{2,1,0:T(8,128)(2,1)}, bf16[8,16,1280]{2,1,0:T(8,128)(2,1)}, bf16[8,16,768]{2,1,0:T(8,128)(2,1)}, bf16[8,16,768]{2,1,0:T(8,128)(2...) custom-call(f32[8,8]{1,0:T(8,128)} %coeffs.1, ...), custom_call_target="tpu_custom_call" | custom-call | tf_op jit(solution)/shard_map/pallas_call | solution.py:550
  160.4 1.1 slice_multiply_fusion
  161.5 0.1 copy.28
  161.6 0.3 mul.71
  161.9 4.9 %copy.29 = f32[2,1,16,4,16,4,4]{3,2,6,5,4,0,1:T(8,128)} copy(f32[2,1,16,4,16,4,4]{4,2,6,5,3,0,1:T(8,128)S(1)} %bitcast.20) | data formatting | bytes 262144 | tf_op jit(solution)/shard_map/vmap()/mul | solution.py:77
  166.9 3.6 %mul.73 = f32[2,1,64,256]{2,3,0,1:T(8,128)S(1)} reshape(f32[2,1,16,4,16,4,4]{3,2,6,5,4,0,1:T(8,128)} %copy.29) | data formatting | bytes 262144 | tf_op jit(solution)/shard_map/vmap()/mul | solution.py:77
  170.5 0.1 copy.21
  170.7 0.8 copy.30
  (1 shorter events, 0.0 us)
Async XLA Ops:
  1.8 4.2 %copy-start = (f32[8,64,168]{2,1,0:T(8,128)S(1)}, f32[8,64,168]{2,1,0:T(8,128)}, u32[]{:S(2)}) copy-start(f32[8,64,168]{2,1,0:T(8,128)} %param.7) | copy-start | bytes 1032196
  3.0 3.2 %copy-start.1 = (f32[8,168,64]{1,2,0:T(8,128)S(1)}, f32[8,168,64]{1,2,0:T(8,128)}, u32[]{:S(2)}) copy-start(f32[8,168,64]{1,2,0:T(8,128)} %param.10) | copy-start | bytes 1032196
  6.5 1.1 slice-start
  6.5 1.3 slice-start.1

commit v4 on v3

--- a/solution.py
+++ b/solution.py
@@ -79,7 +79,7 @@
 
 LANES = 128
 SUB = 8
-PIECE = 256
+PIECE = 512
 
 
 def cut(width, pieces):
@@ -142,7 +142,7 @@
     (feed,) = take(1)
     away, keep, near, over, far = (take(total) for _ in range(5))
     g_send, g_recv, q_send, q_recv = (take(maps) for _ in range(4))
-    (aux_all, proj_w, proj_sq, proj_sq_in, unit_rows, out_rows) = take(6)
+    (aux_all, proj_w, proj_sq, proj_sq_in, unit_rows, out_rows, spread) = take(7)
     (feed_sem, near_sems, far_sems, map_sems, aux_sems, sq_sems, m_sems) = take(7)
 
     rows = groups * 2 * SUB
@@ -235,6 +235,14 @@
 
     pairs = (snap, across, sibling, lax.rem(sibling + 2, 4))
 
+    count = feed.shape[1]
+    for pair in range(4):
+        for which in range(2):
+            for s in range(count):
+                spread[2 * pair + which, s] = jnp.full(
+                    (SUB, LANES), coeffs[s, 2 * pairs[pair] + which], jnp.float32
+                )
+
     def contract(index):
         width = cuts[index]
         slot = index % 2
@@ -243,20 +251,29 @@
             at = pl.ds(pl.multiple_of(group * SUB, SUB), SUB)
             to = pl.ds(pl.multiple_of(group * 2 * SUB, 2 * SUB), 2 * SUB)
             for start in range(0, width, PIECE):
-                lanes = slice(start, min(start + PIECE, width))
-                snaps = [feed[slot, s, at, lanes] for s in range(feed.shape[1])]
+                pieces = [
+                    slice(lane, lane + LANES)
+                    for lane in range(start, min(start + PIECE, width), LANES)
+                ]
+                snaps = [[feed[slot, s, at, piece] for piece in pieces] for s in range(count)]
                 for pair in range(4):
                     both = []
-                    for column in (2 * pairs[pair], 2 * pairs[pair] + 1):
-                        value = coeffs[0, column] * snaps[0]
-                        for s in range(1, len(snaps)):
-                            value = value + coeffs[s, column] * snaps[s]
-                        both.append(value)
-                    packed = jnp.concatenate(both, axis=0).astype(jnp.bfloat16)
-                    if pair < 2:
-                        keep[index][pair, to, lanes] = packed
-                    else:
-                        away[index][pair - 2, to, lanes] = packed
+                    for column in (2 * pair, 2 * pair + 1):
+                        factor = spread[column, 0]
+                        values = [factor * snap_piece for snap_piece in snaps[0]]
+                        for s in range(1, count):
+                            factor = spread[column, s]
+                            values = [
+                                value + factor * snap_piece
+                                for value, snap_piece in zip(values, snaps[s])
+                            ]
+                        both.append(values)
+                    for piece, first, second in zip(pieces, *both):
+                        packed = jnp.concatenate([first, second], axis=0).astype(jnp.bfloat16)
+                        if pair < 2:
+                            keep[index][pair, to, piece] = packed
+                        else:
+                            away[index][pair - 2, to, piece] = packed
             return carry
 
         lax.fori_loop(0, groups, body, 0)
@@ -538,6 +555,7 @@
         pltpu.VMEM((n, 2, 1, proj_wide), wide),
         pltpu.VMEM((both, LANES), kind),
         pltpu.VMEM((2, n * real, LANES), kind),
+        pltpu.VMEM((coeffs.shape[1], snaps, SUB, LANES), wide),
         pltpu.SemaphoreType.DMA((2, 3)),
         pltpu.SemaphoreType.DMA((2, total)),
         pltpu.SemaphoreType.DMA((2, total)),
@@ -589,7 +607,7 @@
     half = LANES // 2
     if fused:
         feature = feature[:, :, half:] / jnp.sqrt(0.58)
-        return jax.vmap(lambda value: finish(value, latent, c_skip, c_out))(feature)
+        return jnp.stack([finish(feature[p], latent, c_skip, c_out) for p in range(owned)])
     maps = [part.reshape(owned, -1, part.shape[2]) for part in maps]
     places = tile_places(plan)
     tiles = []

time: 172 us -> 166 us (0.965)
  Pallas kernels: 151 us -> 148 us
  local copies, waits for them, and re-layouts: 16 us -> 14.1 us
    pallas_call x1, Pallas kernels: 151 us -> 148 us  [exchange_call(): pl.pallas_call(functools.partial(exchange_kernel, plan, tuple(cuts), len(...]
    mul x4 -> x8, local copies, waits for them, and re-layouts: 9 us -> 6.64 us  [finish(): return c_skip[:, None, None] * latent + c_out[:, None, None] * image]
where the time goes in v4:
time: 166 us
  Pallas kernels  148 us (89%)
  local copies, waits for them, and re-layouts  14.1 us (8%)
  other arithmetic  2.86 us (2%)
    pallas_call x1, Pallas kernels, exchange_call(): pl.pallas_call(functools.partial(exchange_kernel, plan, tuple(cuts), len(...  148 us
    mul x8, local copies, waits for them, and re-layouts, finish(): return c_skip[:, None, None] * latent + c_out[:, None, None] * image  6.64 us
    convert_element_type x5, local copies, waits for them, and re-layouts, prepare(): to_tokens(c_in[:, None, None] * latent).reshape(count * 256, 64)  4.25 us

profile of v4, /device:TPU:0, one launch (start us, length us, event | category | flops | bytes accessed | tf_op | source)
XLA Modules:
  0.0 165.6 jit_solution(1482443305144381111)
XLA Ops:
  0.0 0.0 copy-start
  0.0 0.0 copy-start.1
  0.0 1.0 copy-done
  1.0 0.0 slice-start
  1.0 0.0 slice-start.1
  1.0 0.3 copy.26
  1.3 0.0 copy-done.1
  1.3 0.3 copy.25
  1.6 0.6 slice-done
  2.2 0.2 slice-done.1
  2.4 0.0 copy-start.2
  2.4 1.7 %pad_maximum_fusion.aux = f32[8,168,256]{2,1,0:T(8,128)} fusion(f32[8,168,64]{2,1,0:T(8,128)S(1)} %slice-done, f32[8,168,64]{2,1,0:T(8,128)S(1)} %slice-done.1, f32[8,168,64]{2,1,0:T(8,128)S(1)} %copy.26, f32[8,168,64]{2,1,0:T(8,128)S(1)} %bitcast.30), kind=kLoop, calls=%fused_computation | loop fusion | flops 1032192 | bytes 2752512 | tf_op jit(solution)/shard_map/concatenate | solution.py:592
  4.9 0.0 copy-done.2
  4.9 0.1 copy.27
  5.0 1.2 convert_element_type.14
  6.2 2.0 %copy.28 = bf16[1,16,16,4,4,4]{2,1,5,4,3,0:T(8,128)(2,1)S(1)} copy(bf16[1,16,16,4,4,4]{3,1,5,4,2,0:T(8,128)(2,1)S(1)} %bitcast.29) | data formatting | bytes 65536 | tf_op jit(solution)/shard_map/convert_element_type | solution.py:70
  8.2 0.2 convert_element_type.16
  8.4 0.7 copy.29.tokens
  9.2 147.5 %shard_map.73 = (bf16[8,16,128]{2,1,0:T(8,128)(2,1)}, bf16[8,16,1280]{2,1,0:T(8,128)(2,1)}, bf16[8,16,768]{2,1,0:T(8,128)(2,1)}, bf16[8,16,768]{2,1,0:T(8,128)(2...) custom-call(f32[8,8]{1,0:T(8,128)} %coeffs.1, ...), custom_call_target="tpu_custom_call" | custom-call | tf_op jit(solution)/shard_map/pallas_call | solution.py:568
  156.7 1.1 slice_multiply_fusion
  157.9 0.1 copy.31
  158.0 0.2 mul.95
  158.2 2.0 %copy.32 = f32[1,16,4,16,4,4]{2,1,5,4,3,0:T(8,128)S(1)} copy(f32[1,16,4,16,4,4]{3,1,5,4,2,0:T(8,128)S(1)} %bitcast.31) | data formatting | bytes 131072 | tf_op jit(solution)/shard_map/mul | solution.py:77
  160.2 1.0 mul.97
  161.2 0.1 copy.24
  161.4 0.1 copy.34
  161.5 0.2 mul.99
  161.7 2.0 %copy.35 = f32[1,16,4,16,4,4]{2,1,5,4,3,0:T(8,128)S(1)} copy(f32[1,16,4,16,4,4]{3,1,5,4,2,0:T(8,128)S(1)} %bitcast.32) | data formatting | bytes 131072 | tf_op jit(solution)/shard_map/mul | solution.py:77
  163.7 1.0 mul.101
  164.8 0.8 copy.36
  (4 shorter events, 0.1 us)
Async XLA Ops:
  0.0 1.0 copy-start
  0.0 1.3 copy-start.1
  1.0 1.1 slice-start
  1.0 1.4 slice-start.1
  2.4 2.5 %copy-start.2 = (f32[1,64,256]{2,1,0:T(8,128)S(1)}, f32[1,64,256]{2,1,0:T(8,128)}, u32[]{:S(2)}) copy-start(f32[1,64,256]{2,1,0:T(8,128)} %param.12) | copy-start | bytes 196612

commit v5 on v4

--- a/solution.py
+++ b/solution.py
@@ -454,32 +454,58 @@
 
         def body(profile, carry):
             found = {}
+            row = lax.broadcasted_iota(jnp.int32, (LANES, LANES), 0) // HEAD_DIM
+            lane = lax.broadcasted_iota(jnp.int32, (LANES, LANES), 1) // HEAD_DIM
+            same = jnp.where(row == lane, 1.0 / HEAD_DIM, 0.0).astype(jnp.bfloat16)
 
             def unit(column):
-                tile, lane = column // LANES, column % LANES
+                tile, start = column // LANES, column % LANES
                 if tile not in found:
-                    found[tile] = product_of(*places[tile], profile)
+                    own = product_of(*places[tile], profile)
+                    squares = own * own
+                    high = squares.astype(jnp.bfloat16)
+                    low = (squares - high.astype(jnp.float32)).astype(jnp.bfloat16)
+                    mean = jnp.dot(high, same, preferred_element_type=jnp.float32)
+                    mean = mean + jnp.dot(low, same, preferred_element_type=jnp.float32)
+                    found[tile] = own * (1.0 / (EPS + jnp.sqrt(mean)))
                 if tile == len(places) - 1:
-                    lane = LANES // 2
-                own = found[tile][:, lane:lane + HEAD_DIM]
-                scale = jnp.sqrt(jnp.mean(own * own, axis=1, keepdims=True))
-                return (own * (1.0 / (EPS + scale))).astype(jnp.bfloat16)
-
+                    start = LANES // 2
+                return found[tile], start
+
+            queries, keys, values, ends = [], [], [], []
+            for head in heads:
+                own, start = unit(head * HEAD_DIM)
+                own = own[:, start:start + HEAD_DIM] * (1.0 / HEAD_DIM**0.5)
+                queries.append(own.astype(jnp.bfloat16))
+                own, start = unit((count + head) * HEAD_DIM)
+                keys.append(own[:, start:start + HEAD_DIM].astype(jnp.bfloat16))
+                own, start = unit((2 * count + head) * HEAD_DIM)
+                side = lax.broadcasted_iota(jnp.int32, own.shape, 1) // HEAD_DIM
+                own = jnp.where(side == start // HEAD_DIM, own, 1.0)
+                values.append(own.astype(jnp.bfloat16))
+                ends.append(start)
+            expo = [
+                jnp.exp(
+                    lax.dot_general(
+                        query, key, (((1,), (1,)), ((), ())), preferred_element_type=jnp.float32
+                    )
+                ).astype(jnp.bfloat16)
+                for query, key in zip(queries, keys)
+            ]
+            sums = [
+                jnp.dot(weight, value, preferred_element_type=jnp.float32)
+                for weight, value in zip(expo, values)
+            ]
+            mixed = [
+                (value * (1.0 / pltpu.roll(value, HEAD_DIM, 1)))[:, start:start + HEAD_DIM]
+                for value, start in zip(sums, ends)
+            ]
             added = jnp.zeros(feature.shape[1:], jnp.float32)
-            for head in heads:
-                query, keys, values = (
-                    unit((part * count + head) * HEAD_DIM) for part in range(3)
+            for head, value in zip(heads, mixed):
+                rows_of = out_rows[profile, head * HEAD_DIM:(head + 1) * HEAD_DIM, :]
+                added = added + jnp.dot(
+                    value.astype(jnp.bfloat16), rows_of, preferred_element_type=jnp.float32
                 )
-                scores = lax.dot_general(
-                    query, keys, (((1,), (1,)), ((), ())), preferred_element_type=jnp.float32
-                )
-                expo = jnp.exp(scores * (1.0 / HEAD_DIM**0.5))
-                weights = expo * (1.0 / jnp.sum(expo, axis=1, keepdims=True))
-                mixed = jnp.dot(
-                    weights.astype(jnp.bfloat16), values, preferred_element_type=jnp.float32
-                ).astype(jnp.bfloat16)
-                rows_of = out_rows[profile, head * HEAD_DIM:(head + 1) * HEAD_DIM, :]
-                added = added + jnp.dot(mixed, rows_of, preferred_element_type=jnp.float32)
             feature[profile] = feature[profile] + 0.3 * added
             return carry
 

time: 166 us -> 151 us (0.910)
  Pallas kernels: 148 us -> 132 us
    pallas_call x1, Pallas kernels: 148 us -> 132 us  [exchange_call(): pl.pallas_call(functools.partial(exchange_kernel, plan, tuple(cuts), len(...]
where the time goes in v5:
time: 151 us; the launch traced here: 150 us
  Pallas kernels  132 us (87%)
  local copies, waits for them, and re-layouts  14.1 us (9%)
  other arithmetic  2.86 us (2%)
    pallas_call x1, Pallas kernels, exchange_call(): pl.pallas_call(functools.partial(exchange_kernel, plan, tuple(cuts), len(...  132 us
    mul x8, local copies, waits for them, and re-layouts, finish(): return c_skip[:, None, None] * latent + c_out[:, None, None] * image  6.64 us
    convert_element_type x5, local copies, waits for them, and re-layouts, prepare(): to_tokens(c_in[:, None, None] * latent).reshape(count * 256, 64)  4.25 us

profile of v5, /device:TPU:0, one launch (start us, length us, event | category | flops | bytes accessed | tf_op | source)
XLA Modules:
  0.0 150.3 jit_solution(12683965320659235137)
XLA Ops:
  0.0 0.0 copy-start
  0.0 0.0 copy-start.1
  0.0 1.0 copy-done
  1.0 0.0 slice-start
  1.0 0.0 slice-start.1
  1.0 0.3 copy.26
  1.3 0.0 copy-done.1
  1.3 0.3 copy.25
  1.6 0.6 slice-done
  2.2 0.2 slice-done.1
  2.4 0.0 copy-start.2
  2.4 1.7 %pad_maximum_fusion.aux = f32[8,168,256]{2,1,0:T(8,128)} fusion(f32[8,168,64]{2,1,0:T(8,128)S(1)} %slice-done, f32[8,168,64]{2,1,0:T(8,128)S(1)} %slice-done.1, f32[8,168,64]{2,1,0:T(8,128)S(1)} %copy.26, f32[8,168,64]{2,1,0:T(8,128)S(1)} %bitcast.30), kind=kLoop, calls=%fused_computation | loop fusion | flops 1032192 | bytes 2752512 | tf_op jit(solution)/shard_map/concatenate | solution.py:618
  4.9 0.0 copy-done.2
  4.9 0.1 copy.27
  5.0 1.2 convert_element_type.14
  6.2 2.0 %copy.28 = bf16[1,16,16,4,4,4]{2,1,5,4,3,0:T(8,128)(2,1)S(1)} copy(bf16[1,16,16,4,4,4]{3,1,5,4,2,0:T(8,128)(2,1)S(1)} %bitcast.29) | data formatting | bytes 65536 | tf_op jit(solution)/shard_map/convert_element_type | solution.py:70
  8.2 0.2 convert_element_type.16
  8.4 0.7 copy.29.tokens
  9.2 132.3 %shard_map.73 = (bf16[8,16,128]{2,1,0:T(8,128)(2,1)}, bf16[8,16,1280]{2,1,0:T(8,128)(2,1)}, bf16[8,16,768]{2,1,0:T(8,128)(2,1)}, bf16[8,16,768]{2,1,0:T(8,128)(2...) custom-call(f32[8,8]{1,0:T(8,128)} %coeffs.1, ...), custom_call_target="tpu_custom_call" | custom-call | tf_op jit(solution)/shard_map/pallas_call | solution.py:594
  141.5 1.1 slice_multiply_fusion
  142.7 0.1 copy.31
  142.7 0.2 mul.95
  142.9 2.0 %copy.32 = f32[1,16,4,16,4,4]{2,1,5,4,3,0:T(8,128)S(1)} copy(f32[1,16,4,16,4,4]{3,1,5,4,2,0:T(8,128)S(1)} %bitcast.31) | data formatting | bytes 131072 | tf_op jit(solution)/shard_map/mul | solution.py:77
  145.0 1.0 mul.97
  146.0 0.1 copy.24
  146.1 0.1 copy.34
  146.2 0.2 mul.99
  146.4 2.0 %copy.35 = f32[1,16,4,16,4,4]{2,1,5,4,3,0:T(8,128)S(1)} copy(f32[1,16,4,16,4,4]{3,1,5,4,2,0:T(8,128)S(1)} %bitcast.32) | data formatting | bytes 131072 | tf_op jit(solution)/shard_map/mul | solution.py:77
  148.5 1.0 mul.101
  149.6 0.8 copy.36
  (4 shorter events, 0.1 us)
Async XLA Ops:
  0.0 1.0 copy-start
  0.0 1.3 copy-start.1
  1.0 1.1 slice-start
  1.0 1.4 slice-start.1
  2.4 2.5 %copy-start.2 = (f32[1,64,256]{2,1,0:T(8,128)S(1)}, f32[1,64,256]{2,1,0:T(8,128)}, u32[]{:S(2)}) copy-start(f32[1,64,256]{2,1,0:T(8,128)} %param.12) | copy-start | bytes 196612
